TPU v7x, 32 devices: a whole 2x2x4 slice. The times are simulated.
32 devices in a mesh: aux: 2 (over y), ao: 16 (over z, x, core).
Axes of the slice: x: 2, y: 2, z: 4, core: 2. Of those that a mesh axis runs over, the one named last changes fastest.
Arguments:
- pair_list: int32 [384, 2], P('ao'), may hold values from 0 to 63, as said below
- pair_count: int32 [16], P('ao'), may hold values from 3 to 24, as said below
- tiles: bfloat16 [384, 8, 128, 128], P('ao', 'aux'), may hold values from -6 to 6
- coeff: bfloat16 [8192, 512], P('ao'), may hold values from -0.25 to 0.25
Outputs:
- k_tiles: bfloat16 [384, 128, 128], P('ao', 'aux')
Inputs may be any that keep to these rules, and one draw needn't show every extreme that they name: `pair_list`: each live row of owner o names i among its blocks and i < j < (o + 3) * 4; no live pair repeats; rows past an owner's count repeat that owner's first row. `pair_count`: some owner has exactly 24 live rows.
All inputs are finite; a program needn't handle non-finite values.
Results may differ from a plain program's by a relative error of at most 0.0067.
Values may be sent and summed in bfloat16 or wider, within the bound.
A program may use at most 64 MiB of HBM per device.

v0:
```python
import jax
import jax.numpy as jnp
from jax import lax
from jax.sharding import PartitionSpec as P

BAND = 2


def passed_along(value, axis, steps):
    count = lax.axis_size(axis)
    first, last = (max(0, -steps), min(count, count - steps))
    return lax.ppermute(value, axis, [(source, source + steps) for source in range(first, last)])


def add_block(totals, position, update):
    current = lax.dynamic_index_in_dim(totals, position, 0, keepdims=False)
    return lax.dynamic_update_index_in_dim(totals, current + update, position, 0)


def on_device(pair_list, pair_count, tiles, coeff):
    pair_slots = pair_list.shape[0]
    aux_local = tiles.shape[1]
    block_size = tiles.shape[2]
    orbitals = coeff.shape[1]
    own_blocks = coeff.shape[0] // block_size
    window_blocks = (BAND + 1) * own_blocks
    owner_index = lax.axis_index("ao")
    first_block = owner_index * own_blocks
    live_count = pair_count[0]
    own_coeff = coeff.reshape(own_blocks, block_size, orbitals)
    ahead_coeff = [passed_along(own_coeff, "ao", -distance) for distance in range(1, BAND + 1)]
    window_coeff = jnp.concatenate([own_coeff] + ahead_coeff, 0)

    def accumulate(slot_index, totals):
        pair_row = lax.dynamic_index_in_dim(pair_list, slot_index, 0, keepdims=False)
        left_block = pair_row[0] - first_block
        right_block = pair_row[1] - first_block
        pair_tile = lax.dynamic_index_in_dim(tiles, slot_index, 0, keepdims=False)
        left_coeff = lax.dynamic_index_in_dim(window_coeff, left_block, 0, keepdims=False)
        right_coeff = lax.dynamic_index_in_dim(window_coeff, right_block, 0, keepdims=False)
        to_left = jnp.einsum(
            "pmn,nk->pmk", pair_tile, right_coeff, preferred_element_type=jnp.float32
        )
        to_right = jnp.einsum(
            "pmn,mk->pnk", pair_tile, left_coeff, preferred_element_type=jnp.float32
        )
        totals = add_block(totals, left_block, to_left)
        return add_block(totals, right_block, to_right)

    empty = jnp.zeros((window_blocks, aux_local, block_size, orbitals), jnp.float32)
    totals = lax.fori_loop(0, live_count, accumulate, empty)
    halves = totals.astype(jnp.bfloat16)
    fitted_sum = halves[:own_blocks].astype(jnp.float32)
    for distance in range(1, BAND + 1):
        outgoing = halves[distance * own_blocks : (distance + 1) * own_blocks]
        arriving = passed_along(outgoing, "ao", distance)
        fitted_sum = fitted_sum + arriving.astype(jnp.float32)
    fitted = fitted_sum.astype(jnp.bfloat16)
    ahead_fitted = [passed_along(fitted, "ao", -distance) for distance in range(1, BAND + 1)]
    window_fitted = jnp.concatenate([fitted] + ahead_fitted, 0)

    def contract(slot_index, result):
        pair_row = lax.dynamic_index_in_dim(pair_list, slot_index, 0, keepdims=False)
        left_rows = lax.dynamic_index_in_dim(
            window_fitted, pair_row[0] - first_block, 0, keepdims=False
        )
        right_rows = lax.dynamic_index_in_dim(
            window_fitted, pair_row[1] - first_block, 0, keepdims=False
        )
        pair_tile = jnp.einsum(
            "pmk,pnk->mn", left_rows, right_rows, preferred_element_type=jnp.float32
        )
        return lax.dynamic_update_index_in_dim(result, pair_tile, slot_index, 0)

    partial_tiles = lax.fori_loop(
        0, live_count, contract, jnp.zeros((pair_slots, block_size, block_size), jnp.float32)
    )
    summed = lax.psum_scatter(partial_tiles, "aux", scatter_dimension=1, tiled=True)
    norm_factor = (aux_local * lax.axis_size("aux") * orbitals) ** (-0.5)
    return (summed * norm_factor).astype(jnp.bfloat16)


def solution(mesh):
    in_specs = (P("ao", None), P("ao"), P("ao", "aux", None, None), P("ao", None))
    out_specs = P("ao", "aux", None)
    return jax.shard_map(
        on_device, mesh=mesh, in_specs=in_specs, out_specs=out_specs, check_vma=False
    )
```

profile of v0, /device:TPU:0, one launch (start us, length us, event | category | flops | bytes accessed | tf_op | source)
XLA Modules:
  0.0 564.3 jit_solution(10271049537475566109)
XLA Ops:
  10.5 19.4 %collective-permute-done.1 = bf16[4,128,512]{2,1,0:T(8,128)(2,1)S(1)} collective-permute-done((bf16[4,128,512]{2,1,0:T(8,128)(2,1)}, bf16[4,128,512]{2,1,0:T(8,128)(2,1)S(1)}, u32[]{:S(2)}, u32[]{:S(2)}) %collective-permute-start.1) | collective-permute-done | bytes 524320 | tf_op jit(solution)/shard_map/ppermute | solution.py:12
  31.2 6.1 %broadcast_in_dim.18 = f32[12,4,128,512]{3,2,1,0:T(8,128)} broadcast(f32[]{:T(128)} %constant.57.clone.1), dimensions={} | broadcast | bytes 12582916 | tf_op jit(solution)/shard_map/broadcast_in_dim | solution.py:50
  37.3 232.5 %while.20 = (s32[]{:T(128)}, f32[12,4,128,512]{3,2,1,0:T(8,128)}, s32[]{:T(128)}, s32[24,2]{0,1:T(2,128)S(1)}, s32[]{:T(128)}, /*index=5*/bf16[24,4,128,128]{3,2...) while((s32[]{:T(128)}, f32[12,4,128,512]{3,2,1,0:T(8,128)}, ...), condition=%wide.region_1.2_spmd, body=%wide.region_0.1_spmd.sunk | while | flops 134742032 | bytes 8913199 | solution.py:51
  41.3 2.2 fusion.39
  44.8 2.3 fusion.40
  51.0 2.2 fusion.39
  54.5 2.2 fusion.40
  60.7 2.2 fusion.39
  64.1 2.2 fusion.40
  70.3 2.2 fusion.39
  73.8 2.2 fusion.40
  80.0 2.2 fusion.39
  83.5 2.2 fusion.40
  89.6 2.2 fusion.39
  93.1 2.2 fusion.40
  99.3 2.2 fusion.39
  102.7 2.2 fusion.40
  108.9 2.2 fusion.39
  112.4 2.2 fusion.40
  118.6 2.2 fusion.39
  122.1 2.2 fusion.40
  128.2 2.2 fusion.39
  131.7 2.2 fusion.40
  137.9 2.2 fusion.39
  141.4 2.3 fusion.40
  147.6 2.2 fusion.39
  151.1 2.2 fusion.40
  157.3 2.2 fusion.39
  160.8 2.2 fusion.40
  166.9 2.2 fusion.39
  170.4 2.2 fusion.40
  176.6 2.2 fusion.39
  180.1 2.2 fusion.40
  186.2 2.2 fusion.39
  189.7 2.2 fusion.40
  195.9 2.2 fusion.39
  199.4 2.2 fusion.40
  205.6 2.2 fusion.39
  209.0 2.2 fusion.40
  215.2 2.2 fusion.39
  218.7 2.2 fusion.40
  224.9 2.2 fusion.39
  228.4 2.2 fusion.40
  234.6 2.2 fusion.39
  238.0 2.2 fusion.40
  244.2 2.2 fusion.39
  247.7 2.2 fusion.40
  253.8 2.2 fusion.39
  257.3 2.2 fusion.40
  263.5 2.2 fusion.39
  266.9 2.2 fusion.40
  269.8 5.5 convert_element_type.18
  278.6 2.2 collective-permute-done.2
  280.7 42.7 %collective-permute-done.3 = bf16[4,4,128,512]{3,2,1,0:T(8,128)(2,1)S(1)} collective-permute-done((bf16[4,4,128,512]{3,2,1,0:T(8,128)(2,1)S(1)}, bf16[4,4,128,512]{3,2,1,0:T(8,128)(2,1)S(1)}, u32[]{:S(2)}, u32[]{:S(2)}) %collective-permute-start.3) | collective-permute-done | bytes 2097184 | tf_op jit(solution)/shard_map/ppermute | solution.py:12
  323.5 2.4 add_convert_fusion
  328.4 3.7 collective-permute-done.4
  332.1 67.4 %collective-permute-done.5 = bf16[4,4,128,512]{3,2,1,0:T(8,128)(2,1)} collective-permute-done((bf16[4,4,128,512]{3,2,1,0:T(8,128)(2,1)}, bf16[4,4,128,512]{3,2,1,0:T(8,128)(2,1)}, u32[]{:S(2)}, u32[]{:S(2)}) %collective-permute-start.5) | collective-permute-done | bytes 2097184 | tf_op jit(solution)/shard_map/ppermute | solution.py:12
  399.5 5.4 pad_maximum_fusion
  405.1 99.3 %while.21 = (s32[]{:T(128)}, f32[24,128,128]{2,1,0:T(8,128)S(1)}, s32[]{:T(128)}, s32[24,2]{0,1:T(2,128)S(1)}, s32[]{:T(128)}, /*index=5*/bf16[12,4,128,512]{3,2...) while((s32[]{:T(128)}, f32[24,128,128]{2,1,0:T(8,128)S(1)}, s32[]{:T(128)}, ...), condition=%wide.region_3.4_spmd, body=%wide.region_2.3_spmd.sunk | while | flops 67108880 | bytes 1114387 | solution.py:75
  424.1 1.5 fusion.44
  452.9 1.5 fusion.44
  457.0 1.5 fusion.44
  505.5 49.9 %reduce-scatter.2.cloned.1.call-done = f32[24,64,128]{2,1,0:T(8,128)} async-done(((f32[24,128,128]{2,1,0:T(8,128)}), f32[24,64,128]{2,1,0:T(8,128)}) %reduce-scatter.2.cloned.1.call-update) | async-done | bytes 786448 | tf_op jit(solution)/shard_map/reduce_scatter | solution.py:78
  555.4 2.0 multiply_convert_fusion
  (181 shorter events, 138.2 us)
Async XLA Ops:
  6.5 548.9 %reduce-scatter.2.cloned.1.call-start = ((), (), s32[]{:S(2)}) async-start(), calls=%async_computation.1 | async-start | bytes 2359296 | tf_op jit(solution)/shard_map/reduce_scatter | solution.py:78
  6.5 4.0 collective-permute-start
  7.8 22.1 %collective-permute-start.1 = (bf16[4,128,512]{2,1,0:T(8,128)(2,1)}, bf16[4,128,512]{2,1,0:T(8,128)(2,1)S(1)}, u32[]{:S(2)}, u32[]{:S(2)}) collective-permute-start(bf16[4,128,512]{2,1,0:T(8,128)(2,1)} %bitcast.73), channel_id=1, source_target_pairs={{2,0},{3,1},{4,2},{5,3},{6,4},{7,5},{8,6},{9,7},{10,8},{11,9},{12,... | collective-permute-start | bytes 1572872 | tf_op jit(solution)/shard_map/ppermute | solution.py:12
  31.2 6.1 %copy-start.1 = (s32[24,2]{0,1:T(2,128)S(1)}, s32[24,2]{0,1:T(2,128)}, u32[]{:S(2)}) copy-start(s32[24,2]{0,1:T(2,128)} %param.8) | copy-start | bytes 580
  275.7 5.1 collective-permute-start.2
  277.1 46.4 %collective-permute-start.3 = (bf16[4,4,128,512]{3,2,1,0:T(8,128)(2,1)S(1)}, bf16[4,4,128,512]{3,2,1,0:T(8,128)(2,1)S(1)}, u32[]{:S(2)}, u32[]{:S(2)}) collective-permute-start(bf16[4,4,128,512]{3,2,1,0:T(8,128)(2,1)S(1)} %get-tuple-element.109), channel_id=1, source_target_pairs={{0,2},{1,3},{2,4},{3,5},{4,6},{5,7},{6,8},{7,9},{8,10},{9,11},{10,... | collective-permute-start | bytes 6291464 | tf_op jit(solution)/shard_map/ppermute | solution.py:12
  325.8 6.3 %collective-permute-start.4 = (bf16[4,4,128,512]{3,2,1,0:T(8,128)(2,1)}, bf16[4,4,128,512]{3,2,1,0:T(8,128)(2,1)S(1)}, u32[]{:S(2)}, u32[]{:S(2)}) collective-permute-start(bf16[4,4,128,512]{3,2,1,0:T(8,128)(2,1)} %add_convert_fusion), channel_id=1, source_target_pairs={{1,0},{2,1},{3,2},{4,3},{5,4},{6,5},{7,6},{8,7},{9,8},{10,9},{11,1... | collective-permute-start | bytes 6291464 | tf_op jit(solution)/shard_map/ppermute | solution.py:12
  327.1 72.4 %collective-permute-start.5 = (bf16[4,4,128,512]{3,2,1,0:T(8,128)(2,1)}, bf16[4,4,128,512]{3,2,1,0:T(8,128)(2,1)}, u32[]{:S(2)}, u32[]{:S(2)}) collective-permute-start(bf16[4,4,128,512]{3,2,1,0:T(8,128)(2,1)} %add_convert_fusion), channel_id=1, source_target_pairs={{2,0},{3,1},{4,2},{5,3},{6,4},{7,5},{8,6},{9,7},{10,8},{11,9},{12,... | collective-permute-start | bytes 6291464 | tf_op jit(solution)/shard_map/ppermute | solution.py:12
  504.4 1.2 copy-start
Sparse Core Ops, SparseCore 0:
  505.7 49.7 reduce-scatter.1
where the time goes:
time: 569 us; the launch traced here: 564 us
  waiting for transfers between devices  187 us (33%)
  matrix products  142 us (25%)
  local copies, waits for them, and re-layouts  102 us (18%)
  loops' own time  95.6 us (17%)
  other arithmetic  16.5 us (3%)
  between operations  13.5 us (2%)
  starting transfers between devices  8.02 us (1%)
    ppermute x6, waiting for transfers between devices, passed_along(): lax.ppermute(value, axis, [(source, source + steps) for source in range(f...  137 us
    dynamic_slice x48, local copies, waits for them, and re-layouts, add_block(): current = lax.dynamic_index_in_dim(totals, position, 0, keepdims=False)  62.2 us
    dot_general x24, matrix products, accumulate(): jnp.einsum('pmn,mk->pnk', pair_tile, left_coeff, preferred_element_type=j...  53.5 us
    dot_general x24, matrix products, accumulate(): jnp.einsum('pmn,nk->pmk', pair_tile, right_coeff, preferred_element_type=...  52.2 us
    reduce_scatter x1, waiting for transfers between devices, on_device(): lax.psum_scatter(partial_tiles, 'aux', scatter_dimension=1, tiled=True)  49.9 us
    another operation x1, loops' own time, on_device(): totals = lax.fori_loop(0, live_count, accumulate, empty)  48.4 us
    another operation x1, loops' own time, on_device(): lax.fori_loop(0, live_count, contract, jnp.zeros((pair_slots, block_size,...  47.2 us
    dot_general x24, matrix products, contract(): jnp.einsum('pmk,pnk->mn', left_rows, right_rows, preferred_element_type=j...  36 us
  transfers between devices with their start and end apart: 7, of which 7 were waited for; matrix products, arithmetic and copies ran while one was open for 0% of the time, Pallas kernels for 0%

commit v1 on v0

v1 whole, which is shorter than its diff:
```python
import functools

import jax
import jax.numpy as jnp
from jax import lax
from jax.experimental import pallas as pl
from jax.experimental.pallas import tpu as pltpu
from jax.sharding import PartitionSpec as P

GROUP = 4
REACH = 2
VMEM_LIMIT = 48 * 1024 * 1024


def swapped(value, count, bit):
    return lax.ppermute(value, "ao", [(k, k ^ bit) for k in range(count)])


def shifted(value, count, steps):
    lo, hi = max(0, -steps), min(count, count - steps)
    return lax.ppermute(value, "ao", [(k, k + steps) for k in range(lo, hi)])


def halves_kernel(blocks, info, pairs, *refs):
    tiles = refs[:GROUP]
    own, across, core_pair, ahead_a, ahead_b = refs[GROUP : GROUP + 5]
    keep_ref, send_ref = refs[GROUP + 5 : GROUP + 7]
    tile_v, coeff_v, totals, sems = refs[GROUP + 7 :]
    me = info[0]
    first = info[1]

    def place(source, start, index):
        return pltpu.make_async_copy(
            source, coeff_v.at[pl.ds(start * blocks, blocks)], sems.at[index]
        )

    copies = [
        place(own, me, 0),
        place(across, me ^ 2, 1),
        place(core_pair.at[0], me ^ 1, 2),
        place(core_pair.at[1], me ^ 3, 3),
        place(ahead_a, GROUP + (me & 1), 4),
        place(ahead_b, GROUP + 1 - (me & 1), 5),
    ]
    copies += [
        pltpu.make_async_copy(tiles[d], tile_v.at[d], sems.at[6 + d]) for d in range(GROUP)
    ]
    for copy in copies:
        copy.start()
    totals[...] = jnp.zeros_like(totals)
    for copy in copies:
        copy.wait()

    aux_local = tile_v.shape[2]
    for d in range(GROUP):

        def step(slot, carry):
            left = pairs[d, 2 * slot] - first
            right = pairs[d, 2 * slot + 1] - first
            for aux in range(aux_local):
                tile = tile_v[d, slot, aux]
                totals[left, aux] += lax.dot_general(
                    tile, coeff_v[right], (((1,), (0,)), ((), ())),
                    preferred_element_type=jnp.float32,
                )
                totals[right, aux] += lax.dot_general(
                    tile, coeff_v[left], (((0,), (0,)), ((), ())),
                    preferred_element_type=jnp.float32,
                )
            return carry

        lax.fori_loop(0, info[2 + d], step, 0)

    inside = GROUP * blocks
    keep_ref[...] = totals[:inside]
    send_ref[...] = totals[inside:].astype(send_ref.dtype)


def contract_kernel(blocks, info, pairs, own, ahead, keep_ref, send_ref, window, sems):
    first = info[1]
    inside = GROUP * blocks
    copies = [
        pltpu.make_async_copy(own, window.at[pl.ds(0, inside)], sems.at[0]),
        pltpu.make_async_copy(ahead, window.at[pl.ds(inside, REACH * blocks)], sems.at[1]),
    ]
    for copy in copies:
        copy.start()
    for copy in copies:
        copy.wait()
    aux_local = window.shape[1]
    for d in range(GROUP):
        target = (keep_ref, send_ref)[d & 1]

        def step(slot, carry):
            left = pairs[d, 2 * slot] - first
            right = pairs[d, 2 * slot + 1] - first
            total = None
            for aux in range(aux_local):
                part = lax.dot_general(
                    window[left, aux], window[right, aux], (((1,), (1,)), ((), ())),
                    preferred_element_type=jnp.float32,
                )
                total = part if total is None else total + part
            target[d >> 1, slot] = total.astype(target.dtype)
            return carry

        def blank(slot, carry):
            target[d >> 1, slot] = jnp.zeros(target.shape[2:], target.dtype)
            return carry

        lax.fori_loop(0, info[2 + d], step, 0)
        lax.fori_loop(info[2 + d], target.shape[1], blank, 0)


def on_device(pair_list, pair_count, tiles, coeff):
    slots, aux_all, size, _ = tiles.shape
    orbitals = coeff.shape[1]
    blocks = coeff.shape[0] // size
    owners = lax.axis_size("ao")
    aux_parts = lax.axis_size("aux")
    aux_local = aux_all // GROUP
    owner = lax.axis_index("ao")
    me = owner % GROUP
    first = (owner - me) * blocks
    swap = functools.partial(swapped, count=owners)

    own = coeff.reshape(blocks, size, orbitals)
    across = swap(own, bit=2)
    core_pair = swap(jnp.stack([own, across]), bit=1)
    ahead_a = shifted(jnp.where(me < REACH, own, across), owners, -GROUP)
    ahead_b = swap(ahead_a, bit=1)

    listed = jnp.concatenate([pair_list.reshape(-1), pair_count]).reshape(1, -1)
    lists = jnp.concatenate([listed] + [swap(listed, bit=d) for d in range(1, GROUP)], 0)
    counts = lists[:, 2 * slots]
    info = jnp.concatenate([jnp.stack([me, first]).astype(jnp.int32), counts])

    def part_of(member):
        return lax.dynamic_slice_in_dim(tiles, member * aux_local, aux_local, 1)

    group_tiles = [part_of(me)] + [
        swap(part_of(me ^ d), bit=d) for d in range(1, GROUP)
    ]

    smem = pl.BlockSpec(memory_space=pltpu.SMEM)
    anywhere = pl.BlockSpec(memory_space=pl.ANY)
    vmem = pl.BlockSpec(memory_space=pltpu.VMEM)
    inside, outside = GROUP * blocks, REACH * blocks
    window = inside + outside
    keep, send = pl.pallas_call(
        functools.partial(halves_kernel, blocks),
        out_shape=(
            jax.ShapeDtypeStruct((inside, aux_local, size, orbitals), jnp.float32),
            jax.ShapeDtypeStruct((outside, aux_local, size, orbitals), jnp.bfloat16),
        ),
        in_specs=[smem] * 2 + [anywhere] * (GROUP + 5),
        out_specs=(vmem, vmem),
        scratch_shapes=[
            pltpu.VMEM((GROUP, slots, aux_local, size, size), jnp.bfloat16),
            pltpu.VMEM((window, size, orbitals), jnp.bfloat16),
            pltpu.VMEM((window, aux_local, size, orbitals), jnp.float32),
            pltpu.SemaphoreType.DMA((6 + GROUP,)),
        ],
        compiler_params=pltpu.CompilerParams(vmem_limit_bytes=VMEM_LIMIT),
        name="halves",
    )(info, lists, *group_tiles, own, across, core_pair, ahead_a, ahead_b)

    arrived = shifted(send, owners, GROUP)
    near = (keep[:outside] + arrived.astype(jnp.float32)).astype(jnp.bfloat16)
    fitted = jnp.concatenate([near, keep[outside:].astype(jnp.bfloat16)], 0)
    fitted_ahead = shifted(near, owners, -GROUP)

    kept, sent = pl.pallas_call(
        functools.partial(contract_kernel, blocks),
        out_shape=(
            jax.ShapeDtypeStruct((2, slots, size, size), jnp.float32),
            jax.ShapeDtypeStruct((2, slots, size, size), jnp.bfloat16),
        ),
        in_specs=[smem] * 2 + [anywhere] * 2,
        out_specs=(vmem, vmem),
        scratch_shapes=[
            pltpu.VMEM((window, aux_local, size, orbitals), jnp.bfloat16),
            pltpu.SemaphoreType.DMA((2,)),
        ],
        compiler_params=pltpu.CompilerParams(vmem_limit_bytes=VMEM_LIMIT),
        name="contract",
    )(info, lists, fitted, fitted_ahead)

    both = kept + swap(sent, bit=1).astype(jnp.float32)
    mine = both[0] + swap(both[1].astype(jnp.bfloat16), bit=2).astype(jnp.float32)
    norm_factor = (aux_all * aux_parts * orbitals) ** (-0.5)
    if aux_parts == 2:
        rows = size // 2
        side = lax.axis_index("aux")
        away = lax.dynamic_slice_in_dim(mine, (1 - side) * rows, rows, 1)
        here = lax.dynamic_slice_in_dim(mine, side * rows, rows, 1)
        other = lax.ppermute(away.astype(jnp.bfloat16), "aux", [(0, 1), (1, 0)])
        summed = here + other.astype(jnp.float32)
    else:
        summed = lax.psum_scatter(mine, "aux", scatter_dimension=1, tiled=True)
    return (summed * norm_factor).astype(jnp.bfloat16)


def solution(mesh):
    in_specs = (P("ao", None), P("ao"), P("ao", "aux", None, None), P("ao", None))
    out_specs = P("ao", "aux", None)
    return jax.shard_map(
        on_device, mesh=mesh, in_specs=in_specs, out_specs=out_specs, check_vma=False
    )
```

time: 569 us -> 195 us (0.34)
  the two profiles are of different devices: /device:TPU:0 before, /device:TPU:12 now
where the time goes in v1:
time: 195 us
  waiting for transfers between devices  127 us (65%)
  Pallas kernels  33.7 us (17%)
  other arithmetic  13.2 us (7%)
  starting transfers between devices  12.6 us (6%)
  local copies, waits for them, and re-layouts  8.45 us (4%)
    ppermute x11, waiting for transfers between devices, swapped(): return lax.ppermute(value, 'ao', [(k, k ^ bit) for k in range(count)])  64.9 us
    ppermute x3, waiting for transfers between devices, shifted(): return lax.ppermute(value, 'ao', [(k, k + steps) for k in range(lo, hi)])  51.7 us
    pallas_call x1, Pallas kernels, on_device(): pl.pallas_call(functools.partial(halves_kernel, blocks), out_shape=(jax.S...  19 us
    pallas_call x1, Pallas kernels, on_device(): pl.pallas_call(functools.partial(contract_kernel, blocks), out_shape=(jax...  14.7 us
    ppermute x1, waiting for transfers between devices, on_device(): other = lax.ppermute(away.astype(jnp.bfloat16), 'aux', [(0, 1), (1, 0)])  10.1 us
    ppermute x3, starting transfers between devices, shifted(): return lax.ppermute(value, 'ao', [(k, k + steps) for k in range(lo, hi)])  6.19 us
    ppermute x11, starting transfers between devices, swapped(): return lax.ppermute(value, 'ao', [(k, k ^ bit) for k in range(count)])  6.08 us
  transfers between devices with their start and end apart: 15, of which 9 were waited for; matrix products, arithmetic and copies ran while one was open for 4% of the time, Pallas kernels for 0%

profile of v1, /device:TPU:12, one launch (start us, length us, event | category | flops | bytes accessed | tf_op | source)
XLA Modules:
  0.0 195.5 jit_solution(7310661965186842937)
XLA Ops:
  0.0 1.5 collective-permute-start.6
  1.5 0.8 copy.6
  2.2 0.1 reshape.10
  3.0 10.9 %collective-permute-done.6.refs_5_ = bf16[4,128,512]{2,1,0:T(8,128)(2,1)S(1)} collective-permute-done((bf16[4,128,512]{2,1,0:T(8,128)(2,1)}, bf16[4,128,512]{2,1,0:T(8,128)(2,1)S(1)}, u32[]{:S(2)}, u32[]{:S(2)}) %collective-permute-start.6) | collective-permute-done | bytes 524320 | tf_op jit(solution)/shard_map/ppermute | solution.py:16
  13.9 1.9 broadcast_select_fusion
  15.8 2.3 %collective-permute-start.8 = (bf16[4,128,512]{2,1,0:T(8,128)(2,1)}, bf16[4,128,512]{2,1,0:T(8,128)(2,1)}, u32[]{:S(2)}, u32[]{:S(2)}) collective-permute-start(bf16[4,128,512]{2,1,0:T(8,128)(2,1)} %broadcast_select_fusion), channel_id=1, source_target_pairs={{4,0},{5,1},{6,2},{7,3},{8,4},{9,5},{10,6},{11,7},{12,8},{13,9},{1... | collective-permute-start | bytes 1572872 | tf_op jit(solution)/shard_map/ppermute | solution.py:21
  18.1 2.1 %pad_maximum_fusion.1 = bf16[2,4,128,512]{3,2,1,0:T(8,128)(2,1)} fusion(bf16[1,4,128,512]{3,2,1,0:T(8,128)(2,1)S(1)} %bitcast.17, bf16[1,4,128,512]{3,2,1,0:T(8,128)(2,1)} %bitcast.15), kind=kLoop, calls=%fused_computation.7 | loop fusion | flops 524288 | bytes 2097152 | tf_op jit(solution)/shard_map/stack | solution.py:129
  20.3 0.0 collective-permute-start.7
  20.3 0.1 add_bitcast_fusion
  20.3 0.5 collective-permute-start
  20.8 0.5 collective-permute-start.1
  21.3 1.0 collective-permute-start.2
  22.3 0.0 copy-start
  22.3 3.5 %constant_dynamic-slice_fusion = (bf16[24,1,128,128]{3,2,1,0:T(8,128)(2,1)}, bf16[24,1,128,128]{3,2,1,0:T(8,128)(2,1)}, bf16[24,1,128,128]{3,2,1,0:T(8,128)(2,1)S(1)}, bf16[24,1,128,128]{3,2,1,0:T(8,128)(2,1)}) fusion(bf16[24,4,128,128]{3,2,1,0:T(8,128)(2,1)} %param.6, s32[]{:T(128)S(6)} %select_n.37, s32[]{:T(128)S(6)} %select_n.35, s32[]{:T(128)S(6)} %select_n.34, ...), kind=kLoop, calls=%fused_computation.14 | loop fusion | bytes 6291472 | tf_op jit(solution)/shard_map/dynamic_slice | solution.py:139
  25.7 0.0 collective-permute-done
  25.7 0.7 collective-permute-start.3
  26.4 0.0 collective-permute-done.1
  26.4 0.5 collective-permute-start.4
  26.9 0.0 collective-permute-done.2
  26.9 1.0 collective-permute-start.5
  27.9 2.9 %collective-permute-done.8.refs_7_ = bf16[4,128,512]{2,1,0:T(8,128)(2,1)} collective-permute-done((bf16[4,128,512]{2,1,0:T(8,128)(2,1)}, bf16[4,128,512]{2,1,0:T(8,128)(2,1)}, u32[]{:S(2)}, u32[]{:S(2)}) %collective-permute-start.8) | collective-permute-done | bytes 524320 | tf_op jit(solution)/shard_map/ppermute | solution.py:21
  30.8 0.0 collective-permute-start.9
  30.8 0.2 slice_reduce_fusion
  31.0 0.1 pad_add_fusion.1.info
  31.1 0.0 collective-permute-done.3.refs_1_
  31.1 16.0 %collective-permute-done.4.refs_2_ = bf16[24,1,128,128]{3,2,1,0:T(8,128)(2,1)S(1)} collective-permute-done((bf16[24,1,128,128]{3,2,1,0:T(8,128)(2,1)}, bf16[24,1,128,128]{3,2,1,0:T(8,128)(2,1)S(1)}, u32[]{:S(2)}, u32[]{:S(2)}) %collective-permute-start.4) | collective-permute-done | bytes 786464 | tf_op jit(solution)/shard_map/ppermute | solution.py:16
  47.0 15.2 %collective-permute-done.5.refs_3_ = bf16[24,1,128,128]{3,2,1,0:T(8,128)(2,1)} collective-permute-done((bf16[24,1,128,128]{3,2,1,0:T(8,128)(2,1)}, bf16[24,1,128,128]{3,2,1,0:T(8,128)(2,1)}, u32[]{:S(2)}, u32[]{:S(2)}) %collective-permute-start.5) | collective-permute-done | bytes 786464 | tf_op jit(solution)/shard_map/ppermute | solution.py:16
  62.3 0.0 collective-permute-done.9.refs_8_
  62.3 0.0 collective-permute-done.7.refs_6_
  62.3 0.0 copy-done
  62.3 19.0 %halves.1 = (f32[16,1,128,512]{3,2,1,0:T(8,128)}, bf16[8,1,128,512]{3,2,1,0:T(8,128)(2,1)}) custom-call(s32[6]{0:T(128)S(1)} %pad_add_fusion.1.info, s32[4,49]{1,0:T(4,128)S(1)} %pad_add_fusion.pairs, bf16[24,1,128,128]{3,2,1,0:T(8,128)(2,1)S(1)} %get-tuple-element.15.refs_0_, bf16[24,1,128,128]{3,2,1,0:T(8,128)(2,1)S(1)} %collective-permute-done.3.refs_1_, ...), custom_call_target="tpu_custom_call" | custom-call | tf_op jit(solution)/shard_map/halves/pallas_call | solution.py:150
  81.3 1.9 collective-permute-start.10
  83.2 25.9 %collective-permute-done.10 = bf16[8,1,128,512]{3,2,1,0:T(8,128)(2,1)S(1)} collective-permute-done((bf16[8,1,128,512]{3,2,1,0:T(8,128)(2,1)}, bf16[8,1,128,512]{3,2,1,0:T(8,128)(2,1)S(1)}, u32[]{:S(2)}, u32[]{:S(2)}) %collective-permute-start.10) | collective-permute-done | bytes 1048608 | tf_op jit(solution)/shard_map/ppermute | solution.py:21
  109.2 2.0 %add_convert_fusion = bf16[8,1,128,512]{3,2,1,0:T(8,128)(2,1)S(1)} fusion(bf16[8,1,128,512]{3,2,1,0:T(8,128)(2,1)S(1)} %collective-permute-done.10, f32[16,1,128,512]{3,2,1,0:T(8,128)} %get-tuple-element.9), kind=kLoop, calls=%fused_computation.3 | loop fusion | flops 1572864 | bytes 4194304 | tf_op jit(solution)/shard_map/convert_element_type | solution.py:169
  111.2 1.9 collective-permute-start.11
  113.1 1.7 slice.34
  114.8 0.2 pad_maximum_fusion.own
  115.0 22.9 %collective-permute-done.11.ahead = bf16[8,1,128,512]{3,2,1,0:T(8,128)(2,1)S(1)} collective-permute-done((bf16[8,1,128,512]{3,2,1,0:T(8,128)(2,1)S(1)}, bf16[8,1,128,512]{3,2,1,0:T(8,128)(2,1)S(1)}, u32[]{:S(2)}, u32[]{:S(2)}) %collective-permute-start.11) | collective-permute-done | bytes 1048608 | tf_op jit(solution)/shard_map/ppermute | solution.py:21
  137.9 14.7 %contract.1 = (f32[2,24,128,128]{3,2,1,0:T(8,128)}, bf16[2,24,128,128]{3,2,1,0:T(8,128)(2,1)S(1)}) custom-call(s32[6]{0:T(128)S(1)} %pad_add_fusion.1.info, s32[4,49]{1,0:T(4,128)S(1)} %pad_add_fusion.pairs, bf16[16,1,128,512]{3,2,1,0:T(8,128)(2,1)S(1)} %pad_maximum_fusion.own, bf16[8,1,128,512]{3,2,1,0:T(8,128)(2,1)S(1)} %collective-permute-done.11.ahead), custom_call_target="tpu_custom_call" | custom-call | tf_op jit(solution)/shard_map/contract/pallas_call | solution.py:173
  152.6 0.1 collective-permute-start.12
  152.7 3.4 %collective-permute-done.12 = bf16[2,24,128,128]{3,2,1,0:T(8,128)(2,1)S(1)} collective-permute-done((bf16[2,24,128,128]{3,2,1,0:T(8,128)(2,1)S(1)}, bf16[2,24,128,128]{3,2,1,0:T(8,128)(2,1)S(1)}, u32[]{:S(2)}, u32[]{:S(2)}) %collective-permute-start.12) | collective-permute-done | bytes 1572896 | tf_op jit(solution)/shard_map/ppermute | solution.py:16
  156.1 2.3 %convert_add_fusion = f32[2,24,128,128]{3,2,1,0:T(8,128)S(1)} fusion(f32[2,24,128,128]{3,2,1,0:T(8,128)} %get-tuple-element.11, bf16[2,24,128,128]{3,2,1,0:T(8,128)(2,1)S(1)} %collective-permute-done.12), kind=kLoop, calls=%fused_computation | loop fusion | flops 1572864 | bytes 7864320 | tf_op jit(solution)/shard_map/add | solution.py:189
  158.5 1.0 fusion.1
  159.5 0.4 collective-permute-start.13
  159.9 19.5 %collective-permute-done.13 = bf16[24,128,128]{2,1,0:T(8,128)(2,1)} collective-permute-done((bf16[24,128,128]{2,1,0:T(8,128)(2,1)}, bf16[24,128,128]{2,1,0:T(8,128)(2,1)}, u32[]{:S(2)}, u32[]{:S(2)}) %collective-permute-start.13) | collective-permute-done | bytes 786464 | tf_op jit(solution)/shard_map/ppermute | solution.py:16
  179.4 2.5 %fusion = f32[24,128,128]{2,1,0:T(8,128)} fusion(f32[2,24,128,128]{3,2,1,0:T(8,128)S(1)} %convert_add_fusion, bf16[24,128,128]{2,1,0:T(8,128)(2,1)} %collective-permute-done.13), kind=kLoop, calls=%fused_computation.6 | loop fusion | flops 786432 | bytes 3932160 | tf_op jit(solution)/shard_map/add | solution.py:190
  181.9 1.2 dynamic-slice_convert_fusion
  183.1 0.3 collective-permute-start.14
  183.4 10.1 %collective-permute-done.14 = bf16[24,64,128]{2,1,0:T(8,128)(2,1)S(1)} collective-permute-done((bf16[24,64,128]{2,1,0:T(8,128)(2,1)S(1)}, bf16[24,64,128]{2,1,0:T(8,128)(2,1)S(1)}, u32[]{:S(2)}, u32[]{:S(2)}) %collective-permute-start.14) | collective-permute-done | bytes 393248 | tf_op jit(solution)/shard_map/ppermute | solution.py:197
  193.5 2.0 %multiply_convert_fusion = bf16[24,64,128]{2,1,0:T(8,128)(2,1)} fusion(bf16[24,64,128]{2,1,0:T(8,128)(2,1)S(1)} %collective-permute-done.14, f32[24,128,128]{2,1,0:T(8,128)} %fusion, s32[]{:T(128)S(6)} %select_n.40), kind=kLoop, calls=%fused_computation.9 | loop fusion | flops 786432 | bytes 1572868 | tf_op jit(solution)/shard_map/convert_element_type | solution.py:201
  (1 shorter events, 0.0 us)
Async XLA Ops:
  0.0 13.9 %collective-permute-start.6 = (bf16[4,128,512]{2,1,0:T(8,128)(2,1)}, bf16[4,128,512]{2,1,0:T(8,128)(2,1)S(1)}, u32[]{:S(2)}, u32[]{:S(2)}) collective-permute-start(bf16[4,128,512]{2,1,0:T(8,128)(2,1)} %bitcast.13), channel_id=1, source_target_pairs={{0,2},{1,3},{2,0},{3,1},{4,6},{5,7},{6,4},{7,5},{8,10},{9,11},{10,... | collective-permute-start | bytes 1572872 | tf_op jit(solution)/shard_map/ppermute | solution.py:16
  15.8 15.0 %collective-permute-start.8 = (bf16[4,128,512]{2,1,0:T(8,128)(2,1)}, bf16[4,128,512]{2,1,0:T(8,128)(2,1)}, u32[]{:S(2)}, u32[]{:S(2)}) collective-permute-start(bf16[4,128,512]{2,1,0:T(8,128)(2,1)} %broadcast_select_fusion), channel_id=1, source_target_pairs={{4,0},{5,1},{6,2},{7,3},{8,4},{9,5},{10,6},{11,7},{12,8},{13,9},{1... | collective-permute-start | bytes 1572872 | tf_op jit(solution)/shard_map/ppermute | solution.py:21
  20.3 42.0 %collective-permute-start.7 = (bf16[2,4,128,512]{3,2,1,0:T(8,128)(2,1)}, bf16[2,4,128,512]{3,2,1,0:T(8,128)(2,1)}, u32[]{:S(2)}, u32[]{:S(2)}) collective-permute-start(bf16[2,4,128,512]{3,2,1,0:T(8,128)(2,1)} %pad_maximum_fusion.1), channel_id=1, source_target_pairs={{0,1},{1,0},{2,3},{3,2},{4,5},{5,4},{6,7},{7,6},{8,9},{9,8},{10,11... | collective-permute-start | bytes 3145736 | tf_op jit(solution)/shard_map/ppermute | solution.py:16
  20.3 5.4 %collective-permute-start = (s32[1,49]{1,0:T(1,128)S(1)}, s32[1,49]{1,0:T(1,128)S(1)}, u32[]{:S(2)}, u32[]{:S(2)}) collective-permute-start(s32[1,49]{1,0:T(1,128)S(1)} %add_bitcast_fusion), channel_id=1, source_target_pairs={{0,1},{1,0},{2,3},{3,2},{4,5},{5,4},{6,7},{7,6},{8,9},{9,8},{10,11... | collective-permute-start | bytes 596 | tf_op jit(solution)/shard_map/ppermute | solution.py:16
  20.8 5.6 %collective-permute-start.1 = (s32[1,49]{1,0:T(1,128)S(1)}, s32[1,49]{1,0:T(1,128)S(1)}, u32[]{:S(2)}, u32[]{:S(2)}) collective-permute-start(s32[1,49]{1,0:T(1,128)S(1)} %add_bitcast_fusion), channel_id=1, source_target_pairs={{0,2},{1,3},{2,0},{3,1},{4,6},{5,7},{6,4},{7,5},{8,10},{9,11},{10,... | collective-permute-start | bytes 596 | tf_op jit(solution)/shard_map/ppermute | solution.py:16
  21.3 5.6 %collective-permute-start.2 = (s32[1,49]{1,0:T(1,128)S(1)}, s32[1,49]{1,0:T(1,128)S(1)}, u32[]{:S(2)}, u32[]{:S(2)}) collective-permute-start(s32[1,49]{1,0:T(1,128)S(1)} %add_bitcast_fusion), channel_id=1, source_target_pairs={{0,3},{1,2},{2,1},{3,0},{4,7},{5,6},{6,5},{7,4},{8,11},{9,10},{10,... | collective-permute-start | bytes 596 | tf_op jit(solution)/shard_map/ppermute | solution.py:16
  22.3 40.0 %copy-start = (bf16[512,512]{1,0:T(8,128)(2,1)S(1)}, bf16[512,512]{1,0:T(8,128)(2,1)}, u32[]{:S(2)}) copy-start(bf16[512,512]{1,0:T(8,128)(2,1)} %param.7) | copy-start | bytes 1572868
  25.7 5.3 %collective-permute-start.3 = (bf16[24,1,128,128]{3,2,1,0:T(8,128)(2,1)}, bf16[24,1,128,128]{3,2,1,0:T(8,128)(2,1)S(1)}, u32[]{:S(2)}, u32[]{:S(2)}) collective-permute-start(bf16[24,1,128,128]{3,2,1,0:T(8,128)(2,1)} %get-tuple-element.14), channel_id=1, source_target_pairs={{0,1},{1,0},{2,3},{3,2},{4,5},{5,4},{6,7},{7,6},{8,9},{9,8},{10,11... | collective-permute-start | bytes 2359304 | tf_op jit(solution)/shard_map/ppermute | solution.py:16
  26.4 20.6 %collective-permute-start.4 = (bf16[24,1,128,128]{3,2,1,0:T(8,128)(2,1)}, bf16[24,1,128,128]{3,2,1,0:T(8,128)(2,1)S(1)}, u32[]{:S(2)}, u32[]{:S(2)}) collective-permute-start(bf16[24,1,128,128]{3,2,1,0:T(8,128)(2,1)} %get-tuple-element.16), channel_id=1, source_target_pairs={{0,2},{1,3},{2,0},{3,1},{4,6},{5,7},{6,4},{7,5},{8,10},{9,11},{10,... | collective-permute-start | bytes 2359304 | tf_op jit(solution)/shard_map/ppermute | solution.py:16
  26.9 35.4 %collective-permute-start.5 = (bf16[24,1,128,128]{3,2,1,0:T(8,128)(2,1)}, bf16[24,1,128,128]{3,2,1,0:T(8,128)(2,1)}, u32[]{:S(2)}, u32[]{:S(2)}) collective-permute-start(bf16[24,1,128,128]{3,2,1,0:T(8,128)(2,1)} %get-tuple-element.13), channel_id=1, source_target_pairs={{0,3},{1,2},{2,1},{3,0},{4,7},{5,6},{6,5},{7,4},{8,11},{9,10},{10,... | collective-permute-start | bytes 2359304 | tf_op jit(solution)/shard_map/ppermute | solution.py:16
  30.8 31.5 %collective-permute-start.9 = (bf16[4,128,512]{2,1,0:T(8,128)(2,1)}, bf16[4,128,512]{2,1,0:T(8,128)(2,1)}, u32[]{:S(2)}, u32[]{:S(2)}) collective-permute-start(bf16[4,128,512]{2,1,0:T(8,128)(2,1)} %collective-permute-done.8.refs_7_), channel_id=1, source_target_pairs={{0,1},{1,0},{2,3},{3,2},{4,5},{5,4},{6,7},{7,6},{8,9},{9,8},{10,11... | collective-permute-start | bytes 1572872 | tf_op jit(solution)/shard_map/ppermute | solution.py:16
  81.3 27.8 %collective-permute-start.10 = (bf16[8,1,128,512]{3,2,1,0:T(8,128)(2,1)}, bf16[8,1,128,512]{3,2,1,0:T(8,128)(2,1)S(1)}, u32[]{:S(2)}, u32[]{:S(2)}) collective-permute-start(bf16[8,1,128,512]{3,2,1,0:T(8,128)(2,1)} %get-tuple-element.10), channel_id=1, source_target_pairs={{0,4},{1,5},{2,6},{3,7},{4,8},{5,9},{6,10},{7,11},{8,12},{9,13},{1... | collective-permute-start | bytes 3145736 | tf_op jit(solution)/shard_map/ppermute | solution.py:21
  111.2 26.8 %collective-permute-start.11 = (bf16[8,1,128,512]{3,2,1,0:T(8,128)(2,1)S(1)}, bf16[8,1,128,512]{3,2,1,0:T(8,128)(2,1)S(1)}, u32[]{:S(2)}, u32[]{:S(2)}) collective-permute-start(bf16[8,1,128,512]{3,2,1,0:T(8,128)(2,1)S(1)} %add_convert_fusion), channel_id=1, source_target_pairs={{4,0},{5,1},{6,2},{7,3},{8,4},{9,5},{10,6},{11,7},{12,8},{13,9},{1... | collective-permute-start | bytes 3145736 | tf_op jit(solution)/shard_map/ppermute | solution.py:21
  152.6 3.5 %collective-permute-start.12 = (bf16[2,24,128,128]{3,2,1,0:T(8,128)(2,1)S(1)}, bf16[2,24,128,128]{3,2,1,0:T(8,128)(2,1)S(1)}, u32[]{:S(2)}, u32[]{:S(2)}) collective-permute-start(bf16[2,24,128,128]{3,2,1,0:T(8,128)(2,1)S(1)} %get-tuple-element.12), channel_id=1, source_target_pairs={{0,1},{1,0},{2,3},{3,2},{4,5},{5,4},{6,7},{7,6},{8,9},{9,8},{10,11... | collective-permute-start | bytes 4718600 | tf_op jit(solution)/shard_map/ppermute | solution.py:16
  159.5 19.9 %collective-permute-start.13 = (bf16[24,128,128]{2,1,0:T(8,128)(2,1)}, bf16[24,128,128]{2,1,0:T(8,128)(2,1)}, u32[]{:S(2)}, u32[]{:S(2)}) collective-permute-start(bf16[24,128,128]{2,1,0:T(8,128)(2,1)} %fusion.1), channel_id=1, source_target_pairs={{0,2},{1,3},{2,0},{3,1},{4,6},{5,7},{6,4},{7,5},{8,10},{9,11},{10,... | collective-permute-start | bytes 2359304 | tf_op jit(solution)/shard_map/ppermute | solution.py:16
  183.1 10.4 %collective-permute-start.14 = (bf16[24,64,128]{2,1,0:T(8,128)(2,1)S(1)}, bf16[24,64,128]{2,1,0:T(8,128)(2,1)S(1)}, u32[]{:S(2)}, u32[]{:S(2)}) collective-permute-start(bf16[24,64,128]{2,1,0:T(8,128)(2,1)S(1)} %dynamic-slice_convert_fusion), channel_id=1, source_target_pairs={{0,16},{16,0},{1,17},{17,1},{2,18},{18,2},{3,19},{19,3},{4,20},{20... | collective-permute-start | bytes 1179656 | tf_op jit(solution)/shard_map/ppermute | solution.py:197

commit v2 on v1

v2 whole, which is shorter than its diff:
```python
import functools

import jax
import jax.numpy as jnp
from jax import lax
from jax.experimental import pallas as pl
from jax.experimental.pallas import tpu as pltpu
from jax.sharding import PartitionSpec as P

GROUP = 4
REACH = 2
CHUNKS = 2
UNROLL = 4
VMEM_LIMIT = 48 * 1024 * 1024


def swapped(value, count, bit):
    return lax.ppermute(value, "ao", [(k, k ^ bit) for k in range(count)])


def shifted(value, count, steps):
    lo, hi = max(0, -steps), min(count, count - steps)
    return lax.ppermute(value, "ao", [(k, k + steps) for k in range(lo, hi)])


def halves_kernel(blocks, columns, info, pairs, *refs):
    tiles = refs[:GROUP]
    own, across, core_pair, ahead_a, ahead_b = refs[GROUP : GROUP + 5]
    keep_ref, send_ref = refs[GROUP + 5 : GROUP + 7]
    tile_v, coeff_v, totals, sems = refs[GROUP + 7 :]
    me = info[0]
    first = info[1]

    def place(source, start, index):
        return pltpu.make_async_copy(
            source.at[:, :, columns],
            coeff_v.at[pl.ds(start * blocks, blocks)],
            sems.at[index],
        )

    copies = [
        place(own, me, 0),
        place(across, me ^ 2, 1),
        place(core_pair.at[0], me ^ 1, 2),
        place(core_pair.at[1], me ^ 3, 3),
        place(ahead_a, GROUP + (me & 1), 4),
        place(ahead_b, GROUP + 1 - (me & 1), 5),
    ]
    copies += [
        pltpu.make_async_copy(tiles[d], tile_v.at[d], sems.at[6 + d]) for d in range(GROUP)
    ]
    for copy in copies:
        copy.start()
    totals[...] = jnp.zeros_like(totals)
    for copy in copies:
        copy.wait()

    aux_local = tile_v.shape[2]
    for d in range(GROUP):
        count = info[2 + d]

        def step(turn, carry):
            for aux in range(aux_local):
                updates = []
                for k in range(UNROLL):
                    slot = turn * UNROLL + k
                    left = pairs[d, 2 * slot] - first
                    right = pairs[d, 2 * slot + 1] - first
                    tile = tile_v[d, slot, aux]
                    tile = jnp.where(slot < count, tile, jnp.zeros_like(tile))
                    to_left = lax.dot_general(
                        tile, coeff_v[right], (((1,), (0,)), ((), ())),
                        preferred_element_type=jnp.float32,
                    )
                    to_right = lax.dot_general(
                        tile, coeff_v[left], (((0,), (0,)), ((), ())),
                        preferred_element_type=jnp.float32,
                    )
                    updates += [(left, to_left), (right, to_right)]
                for block, update in updates:
                    totals[block, aux] += update
            return carry

        lax.fori_loop(0, (count + UNROLL - 1) // UNROLL, step, 0)

    inside = GROUP * blocks
    keep_ref[...] = totals[:inside]
    send_ref[...] = totals[inside:].astype(send_ref.dtype)


def contract_kernel(blocks, earlier, info, pairs, *refs):
    own, ahead = refs[:2]
    before = refs[2:4] if earlier else None
    keep_ref, send_ref, window, sems = refs[-4:]
    first = info[1]
    inside = GROUP * blocks
    copies = [
        pltpu.make_async_copy(own, window.at[pl.ds(0, inside)], sems.at[0]),
        pltpu.make_async_copy(ahead, window.at[pl.ds(inside, REACH * blocks)], sems.at[1]),
    ]
    for copy in copies:
        copy.start()
    for copy in copies:
        copy.wait()
    aux_local = window.shape[1]
    for d in range(GROUP):
        target = (keep_ref, send_ref)[d & 1]
        base = before[d & 1] if earlier else None
        count = info[2 + d]

        def step(turn, carry):
            results = []
            for k in range(UNROLL):
                slot = turn * UNROLL + k
                left = pairs[d, 2 * slot] - first
                right = pairs[d, 2 * slot + 1] - first
                total = base[d >> 1, slot] if earlier else None
                for aux in range(aux_local):
                    part = lax.dot_general(
                        window[left, aux], window[right, aux], (((1,), (1,)), ((), ())),
                        preferred_element_type=jnp.float32,
                    )
                    total = part if total is None else total + part
                total = jnp.where(slot < count, total, jnp.zeros_like(total))
                results.append((slot, total))
            for slot, total in results:
                target[d >> 1, slot] = total.astype(target.dtype)
            return carry

        def blank(turn, carry):
            for k in range(UNROLL):
                target[d >> 1, turn * UNROLL + k] = jnp.zeros(target.shape[2:], target.dtype)
            return carry

        turns = (count + UNROLL - 1) // UNROLL
        lax.fori_loop(0, turns, step, 0)
        lax.fori_loop(turns, target.shape[1] // UNROLL, blank, 0)


def on_device(pair_list, pair_count, tiles, coeff):
    slots, aux_all, size, _ = tiles.shape
    orbitals = coeff.shape[1]
    blocks = coeff.shape[0] // size
    owners = lax.axis_size("ao")
    aux_parts = lax.axis_size("aux")
    aux_local = aux_all // GROUP
    owner = lax.axis_index("ao")
    me = owner % GROUP
    first = (owner - me) * blocks
    swap = functools.partial(swapped, count=owners)

    def part_of(member):
        return lax.dynamic_slice_in_dim(tiles, member * aux_local, aux_local, 1)

    own = coeff.reshape(blocks, size, orbitals)
    parts, own = lax.optimization_barrier(([part_of(me ^ d) for d in range(GROUP)], own))
    group_tiles = parts[:1] + [swap(parts[d], bit=d) for d in range(1, GROUP)]
    across, group_tiles[2] = lax.optimization_barrier((swap(own, bit=2), group_tiles[2]))
    core_pair = swap(jnp.stack([own, across]), bit=1)
    ahead_a = shifted(jnp.where(me < REACH, own, across), owners, -GROUP)
    ahead_b = swap(ahead_a, bit=1)

    listed = jnp.concatenate([pair_list.reshape(-1), pair_count]).reshape(1, -1)
    lists = jnp.concatenate([listed] + [swap(listed, bit=d) for d in range(1, GROUP)], 0)
    counts = lists[:, 2 * slots]
    info = jnp.concatenate([jnp.stack([me, first]).astype(jnp.int32), counts])

    smem = pl.BlockSpec(memory_space=pltpu.SMEM)
    anywhere = pl.BlockSpec(memory_space=pl.ANY)
    vmem = pl.BlockSpec(memory_space=pltpu.VMEM)
    inside, outside = GROUP * blocks, REACH * blocks
    window = inside + outside
    width = orbitals // CHUNKS

    def halves(chunk):
        columns = slice(chunk * width, (chunk + 1) * width)
        return pl.pallas_call(
            functools.partial(halves_kernel, blocks, columns),
            out_shape=(
                jax.ShapeDtypeStruct((inside, aux_local, size, width), jnp.float32),
                jax.ShapeDtypeStruct((outside, aux_local, size, width), jnp.bfloat16),
            ),
            in_specs=[smem] * 2 + [anywhere] * (GROUP + 5),
            out_specs=(vmem, vmem),
            scratch_shapes=[
                pltpu.VMEM((GROUP, slots, aux_local, size, size), jnp.bfloat16),
                pltpu.VMEM((window, size, width), jnp.bfloat16),
                pltpu.VMEM((window, aux_local, size, width), jnp.float32),
                pltpu.SemaphoreType.DMA((6 + GROUP,)),
            ],
            compiler_params=pltpu.CompilerParams(vmem_limit_bytes=VMEM_LIMIT),
            cost_estimate=pl.CostEstimate(
                flops=8 * GROUP * slots * aux_local * size * size * width,
                bytes_accessed=32 * 1024 * 1024,
                transcendentals=0,
            ),
            name="halves",
        )(info, lists, *group_tiles, own, across, core_pair, ahead_a, ahead_b)

    def contract(fitted, fitted_ahead, before):
        last = len(before) > 0
        return pl.pallas_call(
            functools.partial(contract_kernel, blocks, last),
            out_shape=(
                jax.ShapeDtypeStruct((2, slots, size, size), jnp.float32),
                jax.ShapeDtypeStruct(
                    (2, slots, size, size), jnp.bfloat16 if last else jnp.float32
                ),
            ),
            in_specs=[smem] * 2 + [anywhere] * 2 + [vmem] * len(before),
            out_specs=(vmem, vmem),
            scratch_shapes=[
                pltpu.VMEM((window, aux_local, size, width), jnp.bfloat16),
                pltpu.SemaphoreType.DMA((2,)),
            ],
            compiler_params=pltpu.CompilerParams(vmem_limit_bytes=VMEM_LIMIT),
            cost_estimate=pl.CostEstimate(
                flops=4 * GROUP * slots * aux_local * size * size * width,
                bytes_accessed=32 * 1024 * 1024,
                transcendentals=0,
            ),
            name="contract",
        )(info, lists, fitted, fitted_ahead, *before)

    keep0, send0 = halves(0)
    arrived0 = shifted(send0, owners, GROUP)
    keep1, send1 = halves(1)
    arrived0, keep1, send1 = lax.optimization_barrier((arrived0, keep1, send1))

    def finish(keep, arrived):
        near = (keep[:outside] + arrived.astype(jnp.float32)).astype(jnp.bfloat16)
        return near, jnp.concatenate([near, keep[outside:].astype(jnp.bfloat16)], 0)

    arrived1 = shifted(send1, owners, GROUP)
    near0, fitted0 = finish(keep0, arrived0)
    ahead0 = shifted(near0, owners, -GROUP)
    near1, fitted1 = finish(keep1, arrived1)
    ahead0, near1, fitted1 = lax.optimization_barrier((ahead0, near1, fitted1))
    ahead1 = shifted(near1, owners, -GROUP)
    before = contract(fitted0, ahead0, ())
    kept, sent = contract(fitted1, ahead1, before)

    norm_factor = (aux_all * aux_parts * orbitals) ** (-0.5)
    both = kept + swap(sent, bit=1).astype(jnp.float32)

    def through_pair(value):
        return value[0] + swap(value[1].astype(jnp.bfloat16), bit=2).astype(jnp.float32)

    if aux_parts == 2:
        rows = size // 2
        side = lax.axis_index("aux")

        def through_aux(value):
            dim = value.ndim - 2
            away = lax.dynamic_slice_in_dim(value, (1 - side) * rows, rows, dim)
            here = lax.dynamic_slice_in_dim(value, side * rows, rows, dim)
            other = lax.ppermute(away.astype(jnp.bfloat16), "aux", [(0, 1), (1, 0)])
            return here + other.astype(jnp.float32)

        cut = slots // 2
        early = through_aux(through_pair(both[:, :cut]))
        late = through_pair(through_aux(both[:, cut:]))
        summed = jnp.concatenate([early, late], 0)
    else:
        summed = lax.psum_scatter(through_pair(both), "aux", scatter_dimension=1, tiled=True)
    return (summed * norm_factor).astype(jnp.bfloat16)


def solution(mesh):
    in_specs = (P("ao", None), P("ao"), P("ao", "aux", None, None), P("ao", None))
    out_specs = P("ao", "aux", None)
    return jax.shard_map(
        on_device, mesh=mesh, in_specs=in_specs, out_specs=out_specs, check_vma=False
    )
```

time: 195 us -> 159 us (0.82)
  the two profiles are of different devices: /device:TPU:12 before, /device:TPU:0 now
where the time goes in v2:
time: 159 us; the launch traced here: 158 us
  waiting for transfers between devices  82.8 us (52%)
  Pallas kernels  31.3 us (20%)
  starting transfers between devices  26.2 us (16%)
  local copies, waits for them, and re-layouts  9.01 us (6%)
  other arithmetic  7.54 us (5%)
    ppermute x12, waiting for transfers between devices, swapped(): return lax.ppermute(value, 'ao', [(k, k ^ bit) for k in range(count)])  48.1 us
    ppermute x5, waiting for transfers between devices, shifted(): return lax.ppermute(value, 'ao', [(k, k + steps) for k in range(lo, hi)])  31.4 us
    pallas_call x2, Pallas kernels, halves(): pl.pallas_call(functools.partial(halves_kernel, blocks, columns), out_sha...  16.8 us
    pallas_call x2, Pallas kernels, contract(): pl.pallas_call(functools.partial(contract_kernel, blocks, last), out_shap...  14.5 us
    ppermute x5, starting transfers between devices, shifted(): return lax.ppermute(value, 'ao', [(k, k + steps) for k in range(lo, hi)])  13 us
    ppermute x12, starting transfers between devices, swapped(): return lax.ppermute(value, 'ao', [(k, k ^ bit) for k in range(count)])  10.1 us
    dynamic_slice x1, local copies, waits for them, and re-layouts, part_of(): return lax.dynamic_slice_in_dim(tiles, member * aux_local, aux_local, 1)  3.37 us
    ppermute x2, waiting for transfers between devices, through_aux(): other = lax.ppermute(away.astype(jnp.bfloat16), 'aux', [(0, 1), (1, 0)])  3.27 us
  transfers between devices with their start and end apart: 19, of which 14 were waited for; matrix products, arithmetic and copies ran while one was open for 4% of the time, Pallas kernels for 9%

profile of v2, /device:TPU:0, one launch (start us, length us, event | category | flops | bytes accessed | tf_op | source)
XLA Modules:
  0.0 157.8 jit_solution(14824817663935873794)
XLA Ops:
  0.0 3.4 %constant_dynamic-slice_fusion = (bf16[24,1,128,128]{3,2,1,0:T(8,128)(2,1)}, bf16[24,1,128,128]{3,2,1,0:T(8,128)(2,1)}, bf16[24,1,128,128]{3,2,1,0:T(8,128)(2,1)S(1)}, bf16[24,1,128,128]{3,2,1,0:T(8,128)(2,1)S(1)}) fusion(bf16[24,4,128,128]{3,2,1,0:T(8,128)(2,1)} %param.6, s32[]{:T(128)S(6)} %select_n.39, s32[]{:T(128)S(6)} %select_n.37, s32[]{:T(128)S(6)} %select_n.36, ...), kind=kLoop, calls=%fused_computation.25 | loop fusion | bytes 6291472 | tf_op jit(solution)/shard_map/dynamic_slice | solution.py:153
  3.4 2.9 %collective-permute-start.5 = (bf16[24,1,128,128]{3,2,1,0:T(8,128)(2,1)S(1)}, bf16[24,1,128,128]{3,2,1,0:T(8,128)(2,1)S(1)}, u32[]{:S(2)}, u32[]{:S(2)}) collective-permute-start(bf16[24,1,128,128]{3,2,1,0:T(8,128)(2,1)S(1)} %get-tuple-element.29), channel_id=1, source_target_pairs={{0,2},{1,3},{2,0},{3,1},{4,6},{5,7},{6,4},{7,5},{8,10},{9,11},{10,... | collective-permute-start | bytes 2359304 | tf_op jit(solution)/shard_map/ppermute | solution.py:18
  6.3 0.1 collective-permute-start.4
  6.4 28.7 %collective-permute-done.4.refs_5_ = bf16[4,128,512]{2,1,0:T(8,128)(2,1)S(1)} collective-permute-done((bf16[4,128,512]{2,1,0:T(8,128)(2,1)S(1)}, bf16[4,128,512]{2,1,0:T(8,128)(2,1)S(1)}, u32[]{:S(2)}, u32[]{:S(2)}) %collective-permute-start.4) | collective-permute-done | bytes 524320 | tf_op jit(solution)/shard_map/ppermute | solution.py:18
  35.1 0.0 collective-permute-done.5.refs_2_
  35.1 0.1 broadcast_select_fusion
  35.2 1.3 collective-permute-start.8
  36.5 1.1 pad_maximum_fusion
  37.6 0.0 collective-permute-start.7
  37.6 0.5 collective-permute-start.3
  38.1 1.4 collective-permute-start.6
  39.4 10.8 %collective-permute-done.8.refs_7_ = bf16[4,128,512]{2,1,0:T(8,128)(2,1)} collective-permute-done((bf16[4,128,512]{2,1,0:T(8,128)(2,1)S(1)}, bf16[4,128,512]{2,1,0:T(8,128)(2,1)}, u32[]{:S(2)}, u32[]{:S(2)}) %collective-permute-start.8) | collective-permute-done | bytes 524320 | tf_op jit(solution)/shard_map/ppermute | solution.py:23
  50.3 0.0 collective-permute-start.9
  50.3 0.1 copy.6
  50.4 0.1 reshape.11
  51.1 0.1 add_bitcast_fusion
  51.2 0.5 collective-permute-start
  51.7 0.8 collective-permute-done
  52.5 1.4 collective-permute-start.1
  53.9 4.2 %collective-permute-done.1 = s32[1,49]{1,0:T(1,128)S(1)} collective-permute-done((s32[1,49]{1,0:T(1,128)S(1)}, s32[1,49]{1,0:T(1,128)S(1)}, u32[]{:S(2)}, u32[]{:S(2)}) %collective-permute-start.1) | collective-permute-done | bytes 228 | tf_op jit(solution)/shard_map/ppermute | solution.py:18
  58.1 1.4 collective-permute-start.2
  59.5 1.6 %collective-permute-done.2 = s32[1,49]{1,0:T(1,128)S(1)} collective-permute-done((s32[1,49]{1,0:T(1,128)S(1)}, s32[1,49]{1,0:T(1,128)S(1)}, u32[]{:S(2)}, u32[]{:S(2)}) %collective-permute-start.2) | collective-permute-done | bytes 228 | tf_op jit(solution)/shard_map/ppermute | solution.py:18
  61.1 0.2 slice_reduce_fusion
  61.3 0.1 pad_add_fusion.1.info
  61.3 0.0 collective-permute-done.3.refs_1_
  61.4 0.0 collective-permute-done.6.refs_3_
  61.4 0.0 collective-permute-done.9.refs_8_
  61.4 8.4 %halves.2 = (f32[16,1,128,256]{3,2,1,0:T(8,128)}, bf16[8,1,128,256]{3,2,1,0:T(8,128)(2,1)S(1)}) custom-call(s32[6]{0:T(128)S(1)} %pad_add_fusion.1.info, s32[4,49]{1,0:T(4,128)S(1)} %pad_add_fusion.pairs, bf16[24,1,128,128]{3,2,1,0:T(8,128)(2,1)S(1)} %get-tuple-element.26.refs_0_, bf16[24,1,128,128]{3,2,1,0:T(8,128)(2,1)S(1)} %collective-permute-done.3.refs_1_, ...), custom_call_target="tpu_custom_call" | custom-call | flops 3221225472 | bytes 33554432 | tf_op jit(solution)/shard_map/halves/pallas_call | solution.py:177
  69.8 4.7 %collective-permute-start.10 = (bf16[8,1,128,256]{3,2,1,0:T(8,128)(2,1)S(1)}, bf16[8,1,128,256]{3,2,1,0:T(8,128)(2,1)S(1)}, u32[]{:S(2)}, u32[]{:S(2)}) collective-permute-start(bf16[8,1,128,256]{3,2,1,0:T(8,128)(2,1)S(1)} %get-tuple-element.34), channel_id=1, source_target_pairs={{0,4},{1,5},{2,6},{3,7},{4,8},{5,9},{6,10},{7,11},{8,12},{9,13},{1... | collective-permute-start | bytes 1572872 | tf_op jit(solution)/shard_map/ppermute | solution.py:23
  74.5 8.4 %halves.3 = (f32[16,1,128,256]{3,2,1,0:T(8,128)}, bf16[8,1,128,256]{3,2,1,0:T(8,128)(2,1)S(1)}) custom-call(s32[6]{0:T(128)S(1)} %pad_add_fusion.1.info, s32[4,49]{1,0:T(4,128)S(1)} %pad_add_fusion.pairs, bf16[24,1,128,128]{3,2,1,0:T(8,128)(2,1)S(1)} %get-tuple-element.26.refs_0_, bf16[24,1,128,128]{3,2,1,0:T(8,128)(2,1)S(1)} %collective-permute-done.3.refs_1_, ...), custom_call_target="tpu_custom_call" | custom-call | flops 3221225472 | bytes 33554432 | tf_op jit(solution)/shard_map/halves/pallas_call | solution.py:177
  83.0 2.9 %collective-permute-done.10 = bf16[8,1,128,256]{3,2,1,0:T(8,128)(2,1)S(1)} collective-permute-done((bf16[8,1,128,256]{3,2,1,0:T(8,128)(2,1)S(1)}, bf16[8,1,128,256]{3,2,1,0:T(8,128)(2,1)S(1)}, u32[]{:S(2)}, u32[]{:S(2)}) %collective-permute-start.10) | collective-permute-done | bytes 524320 | tf_op jit(solution)/shard_map/ppermute | solution.py:23
  85.9 4.4 %collective-permute-start.12 = (bf16[8,1,128,256]{3,2,1,0:T(8,128)(2,1)S(1)}, bf16[8,1,128,256]{3,2,1,0:T(8,128)(2,1)S(1)}, u32[]{:S(2)}, u32[]{:S(2)}) collective-permute-start(bf16[8,1,128,256]{3,2,1,0:T(8,128)(2,1)S(1)} %get-tuple-element.39), channel_id=1, source_target_pairs={{0,4},{1,5},{2,6},{3,7},{4,8},{5,9},{6,10},{7,11},{8,12},{9,13},{1... | collective-permute-start | bytes 1572872 | tf_op jit(solution)/shard_map/ppermute | solution.py:23
  90.3 0.1 add_convert_fusion.1
  90.5 1.3 collective-permute-start.11
  91.8 1.3 slice.72
  93.1 7.8 %collective-permute-done.12 = bf16[8,1,128,256]{3,2,1,0:T(8,128)(2,1)S(1)} collective-permute-done((bf16[8,1,128,256]{3,2,1,0:T(8,128)(2,1)S(1)}, bf16[8,1,128,256]{3,2,1,0:T(8,128)(2,1)S(1)}, u32[]{:S(2)}, u32[]{:S(2)}) %collective-permute-start.12) | collective-permute-done | bytes 524320 | tf_op jit(solution)/shard_map/ppermute | solution.py:23
  100.9 0.2 add_convert_fusion
  101.0 0.1 pad_maximum_fusion.1.refs_0_
  101.1 4.6 %collective-permute-done.11.refs_1_ = bf16[8,1,128,256]{3,2,1,0:T(8,128)(2,1)S(1)} collective-permute-done((bf16[8,1,128,256]{3,2,1,0:T(8,128)(2,1)S(1)}, bf16[8,1,128,256]{3,2,1,0:T(8,128)(2,1)S(1)}, u32[]{:S(2)}, u32[]{:S(2)}) %collective-permute-start.11) | collective-permute-done | bytes 524320 | tf_op jit(solution)/shard_map/ppermute | solution.py:23
  105.7 1.3 collective-permute-start.13
  107.0 0.1 slice.71
  107.1 0.1 pad_maximum_fusion.2.refs_0_
  107.2 6.1 %contract.2 = (f32[2,24,128,128]{3,2,1,0:T(8,128)S(1)}, f32[2,24,128,128]{3,2,1,0:T(8,128)}) custom-call(s32[6]{0:T(128)S(1)} %pad_add_fusion.1.info, s32[4,49]{1,0:T(4,128)S(1)} %pad_add_fusion.pairs, bf16[16,1,128,256]{3,2,1,0:T(8,128)(2,1)S(1)} %pad_maximum_fusion.2.refs_0_, bf16[8,1,128,256]{3,2,1,0:T(8,128)(2,1)S(1)} %collective-permute-done.11.refs_1_), custom_call_target="tpu_custom_call" | custom-call | flops 1610612736 | bytes 33554432 | tf_op jit(solution)/shard_map/contract/pallas_call | solution.py:202
  113.3 1.7 %copy-done = f32[2,24,128,128]{3,2,1,0:T(8,128)} copy-done((f32[2,24,128,128]{3,2,1,0:T(8,128)}, f32[2,24,128,128]{3,2,1,0:T(8,128)S(1)}, u32[]{:S(2)}) %copy-start) | copy-done | bytes 3145752
  114.9 5.2 %collective-permute-done.13.refs_1_ = bf16[8,1,128,256]{3,2,1,0:T(8,128)(2,1)S(1)} collective-permute-done((bf16[8,1,128,256]{3,2,1,0:T(8,128)(2,1)S(1)}, bf16[8,1,128,256]{3,2,1,0:T(8,128)(2,1)S(1)}, u32[]{:S(2)}, u32[]{:S(2)}) %collective-permute-start.13) | collective-permute-done | bytes 524320 | tf_op jit(solution)/shard_map/ppermute | solution.py:23
  120.2 8.5 %contract.3 = (f32[2,24,128,128]{3,2,1,0:T(8,128)}, bf16[2,24,128,128]{3,2,1,0:T(8,128)(2,1)S(1)}) custom-call(s32[6]{0:T(128)S(1)} %pad_add_fusion.1.info, s32[4,49]{1,0:T(4,128)S(1)} %pad_add_fusion.pairs, bf16[16,1,128,256]{3,2,1,0:T(8,128)(2,1)S(1)} %pad_maximum_fusion.1.refs_0_, bf16[8,1,128,256]{3,2,1,0:T(8,128)(2,1)S(1)} %collective-permute-done.13.refs_1_, ...), custom_call_target="tpu_custom_call" | custom-call | flops 1610612736 | bytes 33554432 | tf_op jit(solution)/shard_map/contract/pallas_call | solution.py:202
  128.6 0.1 collective-permute-start.14
  128.7 3.4 %collective-permute-done.14 = bf16[2,24,128,128]{3,2,1,0:T(8,128)(2,1)S(1)} collective-permute-done((bf16[2,24,128,128]{3,2,1,0:T(8,128)(2,1)S(1)}, bf16[2,24,128,128]{3,2,1,0:T(8,128)(2,1)S(1)}, u32[]{:S(2)}, u32[]{:S(2)}) %collective-permute-start.14) | collective-permute-done | bytes 1572896 | tf_op jit(solution)/shard_map/ppermute | solution.py:18
  132.1 2.3 %convert_add_fusion = f32[2,24,128,128]{3,2,1,0:T(8,128)S(1)} fusion(f32[2,24,128,128]{3,2,1,0:T(8,128)} %get-tuple-element.45, bf16[2,24,128,128]{3,2,1,0:T(8,128)(2,1)S(1)} %collective-permute-done.14), kind=kLoop, calls=%fused_computation | loop fusion | flops 1572864 | bytes 7864320 | tf_op jit(solution)/shard_map/add | solution.py:244
  134.5 0.1 fusion.2
  134.5 1.6 collective-permute-start.15
  136.1 0.1 slice.51
  136.3 1.2 copy-done.2
  137.4 0.8 dynamic-slice_convert_fusion
  138.3 1.5 collective-permute-start.17
  139.7 6.1 %collective-permute-done.15 = bf16[12,128,128]{2,1,0:T(8,128)(2,1)} collective-permute-done((bf16[12,128,128]{2,1,0:T(8,128)(2,1)S(1)}, bf16[12,128,128]{2,1,0:T(8,128)(2,1)}, u32[]{:S(2)}, u32[]{:S(2)}) %collective-permute-start.15) | collective-permute-done | bytes 393248 | tf_op jit(solution)/shard_map/ppermute | solution.py:18
  145.8 1.1 fusion
  147.0 1.6 %collective-permute-start.16 = (bf16[12,64,128]{2,1,0:T(8,128)(2,1)S(1)}, bf16[12,64,128]{2,1,0:T(8,128)(2,1)S(1)}, u32[]{:S(2)}, u32[]{:S(2)}) collective-permute-start(bf16[12,64,128]{2,1,0:T(8,128)(2,1)S(1)} %dynamic-slice_convert_fusion.1), channel_id=1, source_target_pairs={{0,16},{16,0},{1,17},{17,1},{2,18},{18,2},{3,19},{19,3},{4,20},{20... | collective-permute-start | bytes 589832 | tf_op jit(solution)/shard_map/ppermute | solution.py:257
  148.6 1.2 collective-permute-done.17
  149.8 1.4 convert_add_fusion.1
  151.2 0.3 collective-permute-start.18
  151.5 2.1 %collective-permute-done.16 = bf16[12,64,128]{2,1,0:T(8,128)(2,1)S(1)} collective-permute-done((bf16[12,64,128]{2,1,0:T(8,128)(2,1)S(1)}, bf16[12,64,128]{2,1,0:T(8,128)(2,1)S(1)}, u32[]{:S(2)}, u32[]{:S(2)}) %collective-permute-start.16) | collective-permute-done | bytes 196640 | tf_op jit(solution)/shard_map/ppermute | solution.py:257
  153.6 3.3 %collective-permute-done.18 = bf16[12,64,128]{2,1,0:T(8,128)(2,1)S(1)} collective-permute-done((bf16[12,64,128]{2,1,0:T(8,128)(2,1)S(1)}, bf16[12,64,128]{2,1,0:T(8,128)(2,1)S(1)}, u32[]{:S(2)}, u32[]{:S(2)}) %collective-permute-start.18) | collective-permute-done | bytes 196640 | tf_op jit(solution)/shard_map/ppermute | solution.py:18
  157.0 0.8 fusion.1
  (16 shorter events, 0.2 us)
Async XLA Ops:
  0.0 6.3 %copy-start.1 = (bf16[512,512]{1,0:T(8,128)(2,1)S(1)}, bf16[512,512]{1,0:T(8,128)(2,1)}, u32[]{:S(2)}) copy-start(bf16[512,512]{1,0:T(8,128)(2,1)} %param.7) | copy-start | bytes 1572868
  3.4 46.9 %copy-start.5 = (s32[24,2]{0,1:T(2,128)S(1)}, s32[24,2]{0,1:T(2,128)}, u32[]{:S(2)}) copy-start(s32[24,2]{0,1:T(2,128)} %param.4) | copy-start | bytes 580
  3.4 31.7 %collective-permute-start.5 = (bf16[24,1,128,128]{3,2,1,0:T(8,128)(2,1)S(1)}, bf16[24,1,128,128]{3,2,1,0:T(8,128)(2,1)S(1)}, u32[]{:S(2)}, u32[]{:S(2)}) collective-permute-start(bf16[24,1,128,128]{3,2,1,0:T(8,128)(2,1)S(1)} %get-tuple-element.29), channel_id=1, source_target_pairs={{0,2},{1,3},{2,0},{3,1},{4,6},{5,7},{6,4},{7,5},{8,10},{9,11},{10,... | collective-permute-start | bytes 2359304 | tf_op jit(solution)/shard_map/ppermute | solution.py:18
  6.3 28.8 %collective-permute-start.4 = (bf16[4,128,512]{2,1,0:T(8,128)(2,1)S(1)}, bf16[4,128,512]{2,1,0:T(8,128)(2,1)S(1)}, u32[]{:S(2)}, u32[]{:S(2)}) collective-permute-start(bf16[4,128,512]{2,1,0:T(8,128)(2,1)S(1)} %bitcast.19), channel_id=1, source_target_pairs={{0,2},{1,3},{2,0},{3,1},{4,6},{5,7},{6,4},{7,5},{8,10},{9,11},{10,... | collective-permute-start | bytes 1572872 | tf_op jit(solution)/shard_map/ppermute | solution.py:18
  35.2 15.1 %collective-permute-start.8 = (bf16[4,128,512]{2,1,0:T(8,128)(2,1)S(1)}, bf16[4,128,512]{2,1,0:T(8,128)(2,1)}, u32[]{:S(2)}, u32[]{:S(2)}) collective-permute-start(bf16[4,128,512]{2,1,0:T(8,128)(2,1)S(1)} %broadcast_select_fusion), channel_id=1, source_target_pairs={{4,0},{5,1},{6,2},{7,3},{8,4},{9,5},{10,6},{11,7},{12,8},{13,9},{1... | collective-permute-start | bytes 1572872 | tf_op jit(solution)/shard_map/ppermute | solution.py:23
  37.6 23.8 %collective-permute-start.7 = (bf16[2,4,128,512]{3,2,1,0:T(8,128)(2,1)}, bf16[2,4,128,512]{3,2,1,0:T(8,128)(2,1)}, u32[]{:S(2)}, u32[]{:S(2)}) collective-permute-start(bf16[2,4,128,512]{3,2,1,0:T(8,128)(2,1)} %pad_maximum_fusion), channel_id=1, source_target_pairs={{0,1},{1,0},{2,3},{3,2},{4,5},{5,4},{6,7},{7,6},{8,9},{9,8},{10,11... | collective-permute-start | bytes 3145736 | tf_op jit(solution)/shard_map/ppermute | solution.py:18
  37.6 23.8 %collective-permute-start.3 = (bf16[24,1,128,128]{3,2,1,0:T(8,128)(2,1)}, bf16[24,1,128,128]{3,2,1,0:T(8,128)(2,1)S(1)}, u32[]{:S(2)}, u32[]{:S(2)}) collective-permute-start(bf16[24,1,128,128]{3,2,1,0:T(8,128)(2,1)} %get-tuple-element.27), channel_id=1, source_target_pairs={{0,1},{1,0},{2,3},{3,2},{4,5},{5,4},{6,7},{7,6},{8,9},{9,8},{10,11... | collective-permute-start | bytes 2359304 | tf_op jit(solution)/shard_map/ppermute | solution.py:18
  38.1 23.3 %collective-permute-start.6 = (bf16[24,1,128,128]{3,2,1,0:T(8,128)(2,1)}, bf16[24,1,128,128]{3,2,1,0:T(8,128)(2,1)}, u32[]{:S(2)}, u32[]{:S(2)}) collective-permute-start(bf16[24,1,128,128]{3,2,1,0:T(8,128)(2,1)} %get-tuple-element.31), channel_id=1, source_target_pairs={{0,3},{1,2},{2,1},{3,0},{4,7},{5,6},{6,5},{7,4},{8,11},{9,10},{10,... | collective-permute-start | bytes 2359304 | tf_op jit(solution)/shard_map/ppermute | solution.py:18
  50.3 11.1 %collective-permute-start.9 = (bf16[4,128,512]{2,1,0:T(8,128)(2,1)}, bf16[4,128,512]{2,1,0:T(8,128)(2,1)}, u32[]{:S(2)}, u32[]{:S(2)}) collective-permute-start(bf16[4,128,512]{2,1,0:T(8,128)(2,1)} %collective-permute-done.8.refs_7_), channel_id=1, source_target_pairs={{0,1},{1,0},{2,3},{3,2},{4,5},{5,4},{6,7},{7,6},{8,9},{9,8},{10,11... | collective-permute-start | bytes 1572872 | tf_op jit(solution)/shard_map/ppermute | solution.py:18
  51.2 1.3 collective-permute-start
  52.5 5.6 %collective-permute-start.1 = (s32[1,49]{1,0:T(1,128)S(1)}, s32[1,49]{1,0:T(1,128)S(1)}, u32[]{:S(2)}, u32[]{:S(2)}) collective-permute-start(s32[1,49]{1,0:T(1,128)S(1)} %add_bitcast_fusion), channel_id=1, source_target_pairs={{0,2},{1,3},{2,0},{3,1},{4,6},{5,7},{6,4},{7,5},{8,10},{9,11},{10,... | collective-permute-start | bytes 596 | tf_op jit(solution)/shard_map/ppermute | solution.py:18
  58.1 3.0 %collective-permute-start.2 = (s32[1,49]{1,0:T(1,128)S(1)}, s32[1,49]{1,0:T(1,128)S(1)}, u32[]{:S(2)}, u32[]{:S(2)}) collective-permute-start(s32[1,49]{1,0:T(1,128)S(1)} %add_bitcast_fusion), channel_id=1, source_target_pairs={{0,3},{1,2},{2,1},{3,0},{4,7},{5,6},{6,5},{7,4},{8,11},{9,10},{10,... | collective-permute-start | bytes 596 | tf_op jit(solution)/shard_map/ppermute | solution.py:18
  69.8 20.6 %copy-start.3 = (f32[16,1,128,256]{3,2,1,0:T(8,128)S(1)}, f32[16,1,128,256]{3,2,1,0:T(8,128)}, u32[]{:S(2)}) copy-start(f32[16,1,128,256]{3,2,1,0:T(8,128)} %get-tuple-element.33) | copy-start | bytes 6291460
  69.8 16.1 %collective-permute-start.10 = (bf16[8,1,128,256]{3,2,1,0:T(8,128)(2,1)S(1)}, bf16[8,1,128,256]{3,2,1,0:T(8,128)(2,1)S(1)}, u32[]{:S(2)}, u32[]{:S(2)}) collective-permute-start(bf16[8,1,128,256]{3,2,1,0:T(8,128)(2,1)S(1)} %get-tuple-element.34), channel_id=1, source_target_pairs={{0,4},{1,5},{2,6},{3,7},{4,8},{5,9},{6,10},{7,11},{8,12},{9,13},{1... | collective-permute-start | bytes 1572872 | tf_op jit(solution)/shard_map/ppermute | solution.py:23
  83.0 17.9 %copy-start.4 = (f32[16,1,128,256]{3,2,1,0:T(8,128)S(1)}, f32[16,1,128,256]{3,2,1,0:T(8,128)}, u32[]{:S(2)}) copy-start(f32[16,1,128,256]{3,2,1,0:T(8,128)} %get-tuple-element.38) | copy-start | bytes 6291460
  85.9 14.9 %collective-permute-start.12 = (bf16[8,1,128,256]{3,2,1,0:T(8,128)(2,1)S(1)}, bf16[8,1,128,256]{3,2,1,0:T(8,128)(2,1)S(1)}, u32[]{:S(2)}, u32[]{:S(2)}) collective-permute-start(bf16[8,1,128,256]{3,2,1,0:T(8,128)(2,1)S(1)} %get-tuple-element.39), channel_id=1, source_target_pairs={{0,4},{1,5},{2,6},{3,7},{4,8},{5,9},{6,10},{7,11},{8,12},{9,13},{1... | collective-permute-start | bytes 1572872 | tf_op jit(solution)/shard_map/ppermute | solution.py:23
  90.5 15.3 %collective-permute-start.11 = (bf16[8,1,128,256]{3,2,1,0:T(8,128)(2,1)S(1)}, bf16[8,1,128,256]{3,2,1,0:T(8,128)(2,1)S(1)}, u32[]{:S(2)}, u32[]{:S(2)}) collective-permute-start(bf16[8,1,128,256]{3,2,1,0:T(8,128)(2,1)S(1)} %add_convert_fusion.1), channel_id=1, source_target_pairs={{4,0},{5,1},{6,2},{7,3},{8,4},{9,5},{10,6},{11,7},{12,8},{13,9},{1... | collective-permute-start | bytes 1572872 | tf_op jit(solution)/shard_map/ppermute | solution.py:23
  105.7 14.4 %collective-permute-start.13 = (bf16[8,1,128,256]{3,2,1,0:T(8,128)(2,1)S(1)}, bf16[8,1,128,256]{3,2,1,0:T(8,128)(2,1)S(1)}, u32[]{:S(2)}, u32[]{:S(2)}) collective-permute-start(bf16[8,1,128,256]{3,2,1,0:T(8,128)(2,1)S(1)} %add_convert_fusion), channel_id=1, source_target_pairs={{4,0},{5,1},{6,2},{7,3},{8,4},{9,5},{10,6},{11,7},{12,8},{13,9},{1... | collective-permute-start | bytes 1572872 | tf_op jit(solution)/shard_map/ppermute | solution.py:23
  113.3 1.7 %copy-start = (f32[2,24,128,128]{3,2,1,0:T(8,128)}, f32[2,24,128,128]{3,2,1,0:T(8,128)S(1)}, u32[]{:S(2)}) copy-start(f32[2,24,128,128]{3,2,1,0:T(8,128)S(1)} %get-tuple-element.43.refs_2_) | copy-start | bytes 9437188
  128.6 3.5 %collective-permute-start.14 = (bf16[2,24,128,128]{3,2,1,0:T(8,128)(2,1)S(1)}, bf16[2,24,128,128]{3,2,1,0:T(8,128)(2,1)S(1)}, u32[]{:S(2)}, u32[]{:S(2)}) collective-permute-start(bf16[2,24,128,128]{3,2,1,0:T(8,128)(2,1)S(1)} %get-tuple-element.46), channel_id=1, source_target_pairs={{0,1},{1,0},{2,3},{3,2},{4,5},{5,4},{6,7},{7,6},{8,9},{9,8},{10,11... | collective-permute-start | bytes 4718600 | tf_op jit(solution)/shard_map/ppermute | solution.py:18
  134.5 11.3 %collective-permute-start.15 = (bf16[12,128,128]{2,1,0:T(8,128)(2,1)S(1)}, bf16[12,128,128]{2,1,0:T(8,128)(2,1)}, u32[]{:S(2)}, u32[]{:S(2)}) collective-permute-start(bf16[12,128,128]{2,1,0:T(8,128)(2,1)S(1)} %fusion.2), channel_id=1, source_target_pairs={{0,2},{1,3},{2,0},{3,1},{4,6},{5,7},{6,4},{7,5},{8,10},{9,11},{10,... | collective-permute-start | bytes 1179656 | tf_op jit(solution)/shard_map/ppermute | solution.py:18
  136.3 1.2 copy-start.2
  138.3 11.5 %collective-permute-start.17 = (bf16[2,12,64,128]{3,2,1,0:T(8,128)(2,1)}, bf16[2,12,64,128]{3,2,1,0:T(8,128)(2,1)}, u32[]{:S(2)}, u32[]{:S(2)}) collective-permute-start(bf16[2,12,64,128]{3,2,1,0:T(8,128)(2,1)} %dynamic-slice_convert_fusion), channel_id=1, source_target_pairs={{0,16},{16,0},{1,17},{17,1},{2,18},{18,2},{3,19},{19,3},{4,20},{20... | collective-permute-start | bytes 1179656 | tf_op jit(solution)/shard_map/ppermute | solution.py:257
  147.0 6.6 %collective-permute-start.16 = (bf16[12,64,128]{2,1,0:T(8,128)(2,1)S(1)}, bf16[12,64,128]{2,1,0:T(8,128)(2,1)S(1)}, u32[]{:S(2)}, u32[]{:S(2)}) collective-permute-start(bf16[12,64,128]{2,1,0:T(8,128)(2,1)S(1)} %dynamic-slice_convert_fusion.1), channel_id=1, source_target_pairs={{0,16},{16,0},{1,17},{17,1},{2,18},{18,2},{3,19},{19,3},{4,20},{20... | collective-permute-start | bytes 589832 | tf_op jit(solution)/shard_map/ppermute | solution.py:257
  151.2 5.7 %collective-permute-start.18 = (bf16[12,64,128]{2,1,0:T(8,128)(2,1)S(1)}, bf16[12,64,128]{2,1,0:T(8,128)(2,1)S(1)}, u32[]{:S(2)}, u32[]{:S(2)}) collective-permute-start(bf16[12,64,128]{2,1,0:T(8,128)(2,1)S(1)} %fusion.4), channel_id=1, source_target_pairs={{0,2},{1,3},{2,0},{3,1},{4,6},{5,7},{6,4},{7,5},{8,10},{9,11},{10,... | collective-permute-start | bytes 589832 | tf_op jit(solution)/shard_map/ppermute | solution.py:18

commit v3 on v2

--- a/solution.py
+++ b/solution.py
@@ -88,10 +88,11 @@
     send_ref[...] = totals[inside:].astype(send_ref.dtype)
 
 
-def contract_kernel(blocks, earlier, info, pairs, *refs):
+def contract_kernel(blocks, ranges, earlier, info, pairs, *refs):
     own, ahead = refs[:2]
     before = refs[2:4] if earlier else None
-    keep_ref, send_ref, window, sems = refs[-4:]
+    window, sems = refs[-2:]
+    outs = refs[-2 - 2 * len(ranges) : -2]
     first = info[1]
     inside = GROUP * blocks
     copies = [
@@ -103,38 +104,39 @@
     for copy in copies:
         copy.wait()
     aux_local = window.shape[1]
-    for d in range(GROUP):
-        target = (keep_ref, send_ref)[d & 1]
-        base = before[d & 1] if earlier else None
-        count = info[2 + d]
-
-        def step(turn, carry):
-            results = []
-            for k in range(UNROLL):
-                slot = turn * UNROLL + k
-                left = pairs[d, 2 * slot] - first
-                right = pairs[d, 2 * slot + 1] - first
-                total = base[d >> 1, slot] if earlier else None
-                for aux in range(aux_local):
-                    part = lax.dot_general(
-                        window[left, aux], window[right, aux], (((1,), (1,)), ((), ())),
-                        preferred_element_type=jnp.float32,
-                    )
-                    total = part if total is None else total + part
-                total = jnp.where(slot < count, total, jnp.zeros_like(total))
-                results.append((slot, total))
-            for slot, total in results:
-                target[d >> 1, slot] = total.astype(target.dtype)
-            return carry
-
-        def blank(turn, carry):
-            for k in range(UNROLL):
-                target[d >> 1, turn * UNROLL + k] = jnp.zeros(target.shape[2:], target.dtype)
-            return carry
-
-        turns = (count + UNROLL - 1) // UNROLL
-        lax.fori_loop(0, turns, step, 0)
-        lax.fori_loop(turns, target.shape[1] // UNROLL, blank, 0)
+    for r, (start, length) in enumerate(ranges):
+        for d in range(GROUP):
+            target = outs[2 * r + (d & 1)]
+            base = before[d & 1] if earlier else None
+            count = jnp.clip(info[2 + d] - start, 0, length)
+
+            def step(turn, carry):
+                results = []
+                for k in range(UNROLL):
+                    slot = turn * UNROLL + k
+                    left = pairs[d, 2 * (start + slot)] - first
+                    right = pairs[d, 2 * (start + slot) + 1] - first
+                    total = base[d >> 1, slot] if earlier else None
+                    for aux in range(aux_local):
+                        part = lax.dot_general(
+                            window[left, aux], window[right, aux], (((1,), (1,)), ((), ())),
+                            preferred_element_type=jnp.float32,
+                        )
+                        total = part if total is None else total + part
+                    total = jnp.where(slot < count, total, jnp.zeros_like(total))
+                    results.append((slot, total))
+                for slot, total in results:
+                    target[d >> 1, slot] = total.astype(target.dtype)
+                return carry
+
+            def blank(turn, carry):
+                for k in range(UNROLL):
+                    target[d >> 1, turn * UNROLL + k] = jnp.zeros(target.shape[2:], target.dtype)
+                return carry
+
+            turns = (count + UNROLL - 1) // UNROLL
+            lax.fori_loop(0, turns, step, 0)
+            lax.fori_loop(turns, length // UNROLL, blank, 0)
 
 
 def on_device(pair_list, pair_count, tiles, coeff):
@@ -153,15 +155,16 @@
         return lax.dynamic_slice_in_dim(tiles, member * aux_local, aux_local, 1)
 
     own = coeff.reshape(blocks, size, orbitals)
-    parts, own = lax.optimization_barrier(([part_of(me ^ d) for d in range(GROUP)], own))
-    group_tiles = parts[:1] + [swap(parts[d], bit=d) for d in range(1, GROUP)]
-    across, group_tiles[2] = lax.optimization_barrier((swap(own, bit=2), group_tiles[2]))
+    near_part = swap(part_of(me ^ 1), bit=1)
+    crossing = swap(jnp.stack([part_of(me ^ 2), part_of(me ^ 3)]), bit=2)
+    group_tiles = [part_of(me), near_part, crossing[0], swap(crossing[1], bit=1)]
+    listed = jnp.concatenate([pair_list.reshape(-1), pair_count]).reshape(1, -1)
+    lists = jnp.concatenate([listed] + [swap(listed, bit=d) for d in range(1, GROUP)], 0)
+    across, lists = lax.optimization_barrier((swap(own, bit=2), lists))
     core_pair = swap(jnp.stack([own, across]), bit=1)
     ahead_a = shifted(jnp.where(me < REACH, own, across), owners, -GROUP)
     ahead_b = swap(ahead_a, bit=1)
 
-    listed = jnp.concatenate([pair_list.reshape(-1), pair_count]).reshape(1, -1)
-    lists = jnp.concatenate([listed] + [swap(listed, bit=d) for d in range(1, GROUP)], 0)
     counts = lists[:, 2 * slots]
     info = jnp.concatenate([jnp.stack([me, first]).astype(jnp.int32), counts])
 
@@ -197,18 +200,18 @@
             name="halves",
         )(info, lists, *group_tiles, own, across, core_pair, ahead_a, ahead_b)
 
-    def contract(fitted, fitted_ahead, before):
+    def contract(fitted, fitted_ahead, ranges, before):
         last = len(before) > 0
+        shapes = []
+        for _, length in ranges:
+            shape = (2, length, size, size)
+            shapes.append(jax.ShapeDtypeStruct(shape, jnp.float32))
+            shapes.append(jax.ShapeDtypeStruct(shape, jnp.bfloat16 if last else jnp.float32))
         return pl.pallas_call(
-            functools.partial(contract_kernel, blocks, last),
-            out_shape=(
-                jax.ShapeDtypeStruct((2, slots, size, size), jnp.float32),
-                jax.ShapeDtypeStruct(
-                    (2, slots, size, size), jnp.bfloat16 if last else jnp.float32
-                ),
-            ),
+            functools.partial(contract_kernel, blocks, ranges, last),
+            out_shape=tuple(shapes),
             in_specs=[smem] * 2 + [anywhere] * 2 + [vmem] * len(before),
-            out_specs=(vmem, vmem),
+            out_specs=(vmem,) * len(shapes),
             scratch_shapes=[
                 pltpu.VMEM((window, aux_local, size, width), jnp.bfloat16),
                 pltpu.SemaphoreType.DMA((2,)),
@@ -216,7 +219,7 @@
             compiler_params=pltpu.CompilerParams(vmem_limit_bytes=VMEM_LIMIT),
             cost_estimate=pl.CostEstimate(
                 flops=4 * GROUP * slots * aux_local * size * size * width,
-                bytes_accessed=32 * 1024 * 1024,
+                bytes_accessed=16 * 1024 * 1024,
                 transcendentals=0,
             ),
             name="contract",
@@ -237,11 +240,17 @@
     near1, fitted1 = finish(keep1, arrived1)
     ahead0, near1, fitted1 = lax.optimization_barrier((ahead0, near1, fitted1))
     ahead1 = shifted(near1, owners, -GROUP)
-    before = contract(fitted0, ahead0, ())
-    kept, sent = contract(fitted1, ahead1, before)
+    cut = slots // 2 // UNROLL * UNROLL
+    ranges = [(0, cut), (cut, slots - cut)]
+    before = contract(fitted0, ahead0, ranges, ())
+    kept_a, sent_a = contract(fitted1, ahead1, ranges[:1], before[:2])
+    swapped_a = swap(sent_a, bit=1)
+    kept_b, sent_b = contract(fitted1, ahead1, ranges[1:], before[2:])
+    swapped_a, kept_b, sent_b = lax.optimization_barrier((swapped_a, kept_b, sent_b))
 
     norm_factor = (aux_all * aux_parts * orbitals) ** (-0.5)
-    both = kept + swap(sent, bit=1).astype(jnp.float32)
+    both_a = kept_a + swapped_a.astype(jnp.float32)
+    both_b = kept_b + swap(sent_b, bit=1).astype(jnp.float32)
 
     def through_pair(value):
         return value[0] + swap(value[1].astype(jnp.bfloat16), bit=2).astype(jnp.float32)
@@ -257,11 +266,11 @@
             other = lax.ppermute(away.astype(jnp.bfloat16), "aux", [(0, 1), (1, 0)])
             return here + other.astype(jnp.float32)
 
-        cut = slots // 2
-        early = through_aux(through_pair(both[:, :cut]))
-        late = through_pair(through_aux(both[:, cut:]))
+        early = through_aux(through_pair(both_a))
+        late = through_pair(through_aux(both_b))
         summed = jnp.concatenate([early, late], 0)
     else:
+        both = jnp.concatenate([both_a, both_b], 1)
         summed = lax.psum_scatter(through_pair(both), "aux", scatter_dimension=1, tiled=True)
     return (summed * norm_factor).astype(jnp.bfloat16)
 

time: 159 us -> 162 us (1.019); the launches traced: 158 us -> 163 us
  Pallas kernels: 31.3 us -> 37.8 us
  starting transfers between devices: 26.2 us -> 22.6 us
  waiting for transfers between devices: 82.8 us -> 85 us
    ppermute x12 -> x13, waiting for transfers between devices: 48.1 us -> 52.6 us  [swapped(): return lax.ppermute(value, 'ao', [(k, k ^ bit) for k in range(count)])]
    pallas_call x2, Pallas kernels: 16.8 us -> 21 us  [halves(): pl.pallas_call(functools.partial(halves_kernel, blocks, columns), out_sha...]
    dynamic_slice x1 -> x0, local copies, waits for them, and re-layouts: 3.37 us -> none  [part_of(): return lax.dynamic_slice_in_dim(tiles, member * aux_local, aux_local, 1)]
    another operation x0 -> x1, local copies, waits for them, and re-layouts: none -> 3.02 us  [on_device(): crossing = swap(jnp.stack([part_of(me ^ 2), part_of(me ^ 3)]), bit=2)]
    ppermute x5, starting transfers between devices: 13 us -> 10.3 us  [shifted(): return lax.ppermute(value, 'ao', [(k, k + steps) for k in range(lo, hi)])]
    squeeze x0 -> x1, local copies, waits for them, and re-layouts: none -> 2.44 us  [on_device(): crossing[1]]
    pallas_call x2 -> x3, Pallas kernels: 14.5 us -> 16.8 us  [contract(): pl.pallas_call(functools.partial(contract_kernel, blocks, ranges, last),...]
    ppermute x5, waiting for transfers between devices: 31.4 us -> 29.5 us  [shifted(): return lax.ppermute(value, 'ao', [(k, k + steps) for k in range(lo, hi)])]
  transfers between devices with their start and end apart: 19 -> 20, of which waited for: 14 -> 10; matrix products, arithmetic and copies ran while one was open for 4% -> 6% of each run, Pallas kernels for 9% -> 14%
where the time goes in v3:
time: 162 us; the launch traced here: 163 us
  waiting for transfers between devices  85 us (52%)
  Pallas kernels  37.8 us (23%)
  starting transfers between devices  22.6 us (14%)
  local copies, waits for them, and re-layouts  8.2 us (5%)
  other arithmetic  8.04 us (5%)
    ppermute x13, waiting for transfers between devices, swapped(): return lax.ppermute(value, 'ao', [(k, k ^ bit) for k in range(count)])  52.6 us
    ppermute x5, waiting for transfers between devices, shifted(): return lax.ppermute(value, 'ao', [(k, k + steps) for k in range(lo, hi)])  29.5 us
    pallas_call x2, Pallas kernels, halves(): pl.pallas_call(functools.partial(halves_kernel, blocks, columns), out_sha...  21 us
    pallas_call x3, Pallas kernels, contract(): pl.pallas_call(functools.partial(contract_kernel, blocks, ranges, last),...  16.8 us
    ppermute x5, starting transfers between devices, shifted(): return lax.ppermute(value, 'ao', [(k, k + steps) for k in range(lo, hi)])  10.3 us
    ppermute x13, starting transfers between devices, swapped(): return lax.ppermute(value, 'ao', [(k, k ^ bit) for k in range(count)])  9.17 us
  transfers between devices with their start and end apart: 20, of which 10 were waited for; matrix products, arithmetic and copies ran while one was open for 6% of the time, Pallas kernels for 14%

profile of v3, /device:TPU:0, one launch (start us, length us, event | category | flops | bytes accessed | tf_op | source)
XLA Modules:
  0.0 162.7 jit_solution(13953449477846498635)
XLA Ops:
  0.0 3.0 %dynamic-slice_bitcast_fusion.1 = (bf16[1,24,1,128,128]{4,3,1,2,0:T(8,128)(2,1)S(1)}, bf16[24,1,128,128]{3,2,1,0:T(8,128)(2,1)}, bf16[24,1,128,128]{3,2,1,0:T(8,128)(2,1)S(1)}, bf16[1,24,1,128,128]{4,3,1,2,0:T(8,128)(2,1)S(1)}) fusion(bf16[24,4,128,128]{3,2,1,0:T(8,128)(2,1)} %param.6, s32[]{:T(128)S(6)} %select_n.38, s32[]{:T(128)S(6)} %select_n.37, ...), kind=kLoop, calls=%fused_computation.20 | loop fusion | bytes 6291472 | tf_op jit(solution)/shard_map/stack | solution.py:159
  3.0 1.3 pad_maximum_fusion
  4.3 2.9 %collective-permute-start.5 = (bf16[2,24,1,128,128]{4,3,1,2,0:T(8,128)(2,1)}, bf16[2,24,1,128,128]{4,3,1,2,0:T(8,128)(2,1)}, u32[]{:S(2)}, u32[]{:S(2)}) collective-permute-start(bf16[2,24,1,128,128]{4,3,1,2,0:T(8,128)(2,1)} %pad_maximum_fusion), channel_id=1, source_target_pairs={{0,2},{1,3},{2,0},{3,1},{4,6},{5,7},{6,4},{7,5},{8,10},{9,11},{10,... | collective-permute-start | bytes 4718600 | tf_op jit(solution)/shard_map/ppermute | solution.py:18
  7.2 0.0 collective-permute-start
  7.3 0.1 copy.8
  7.4 0.1 reshape.12
  8.1 0.1 add_bitcast_fusion
  8.2 0.0 collective-permute-start.1
  8.2 2.1 %collective-permute-start.2 = (s32[1,49]{1,0:T(1,128)S(1)}, s32[1,49]{1,0:T(1,128)S(1)}, u32[]{:S(2)}, u32[]{:S(2)}) collective-permute-start(s32[1,49]{1,0:T(1,128)S(1)} %add_bitcast_fusion), channel_id=1, source_target_pairs={{0,2},{1,3},{2,0},{3,1},{4,6},{5,7},{6,4},{7,5},{8,10},{9,11},{10,... | collective-permute-start | bytes 596 | tf_op jit(solution)/shard_map/ppermute | solution.py:18
  10.3 0.1 collective-permute-start.3
  10.3 0.1 collective-permute-start.4
  10.5 42.7 %collective-permute-done.2 = s32[1,49]{1,0:T(1,128)S(1)} collective-permute-done((s32[1,49]{1,0:T(1,128)S(1)}, s32[1,49]{1,0:T(1,128)S(1)}, u32[]{:S(2)}, u32[]{:S(2)}) %collective-permute-start.2) | collective-permute-done | bytes 228 | tf_op jit(solution)/shard_map/ppermute | solution.py:18
  53.2 0.1 broadcast_select_fusion
  53.2 1.3 collective-permute-start.8
  54.5 1.1 pad_maximum_fusion.1
  55.6 0.0 collective-permute-start.7
  55.6 2.4 %slice_bitcast_fusion.1 = (bf16[24,1,128,128]{3,2,1,0:T(8,128)(2,1)}, bf16[24,1,128,128]{3,2,1,0:T(8,128)(2,1)S(1)}) fusion(bf16[2,24,1,128,128]{4,3,1,2,0:T(8,128)(2,1)} %collective-permute-done.5), kind=kLoop, calls=%fused_computation.13 | loop fusion | bytes 3145728 | tf_op jit(solution)/shard_map/squeeze | solution.py:160
  58.1 0.5 collective-permute-start.6
  58.6 10.5 %collective-permute-done.8.refs_7_ = bf16[4,128,512]{2,1,0:T(8,128)(2,1)S(1)} collective-permute-done((bf16[4,128,512]{2,1,0:T(8,128)(2,1)S(1)}, bf16[4,128,512]{2,1,0:T(8,128)(2,1)S(1)}, u32[]{:S(2)}, u32[]{:S(2)}) %collective-permute-start.8) | collective-permute-done | bytes 524320 | tf_op jit(solution)/shard_map/ppermute | solution.py:23
  69.1 0.0 collective-permute-start.9
  69.1 0.2 slice_reduce_fusion
  69.3 0.1 pad_add_fusion.1.info
  69.4 0.0 collective-permute-done.4.refs_1_
  69.4 1.8 %collective-permute-done.9.refs_8_ = bf16[4,128,512]{2,1,0:T(8,128)(2,1)} collective-permute-done((bf16[4,128,512]{2,1,0:T(8,128)(2,1)S(1)}, bf16[4,128,512]{2,1,0:T(8,128)(2,1)}, u32[]{:S(2)}, u32[]{:S(2)}) %collective-permute-start.9) | collective-permute-done | bytes 524320 | tf_op jit(solution)/shard_map/ppermute | solution.py:18
  71.1 0.0 collective-permute-done.6.refs_3_
  71.1 10.5 %halves.2 = (f32[16,1,128,256]{3,2,1,0:T(8,128)}, bf16[8,1,128,256]{3,2,1,0:T(8,128)(2,1)S(1)}) custom-call(s32[6]{0:T(128)S(1)} %pad_add_fusion.1.info, s32[4,49]{1,0:T(4,128)S(1)} %pad_add_fusion.pairs, bf16[24,1,128,128]{3,2,1,0:T(8,128)(2,1)S(1)} %get-tuple-element.53.refs_0_, bf16[24,1,128,128]{3,2,1,0:T(8,128)(2,1)} %collective-permute-done.4.refs_1_, ...), custom_call_target="tpu_custom_call" | custom-call | flops 3221225472 | bytes 33554432 | tf_op jit(solution)/shard_map/halves/pallas_call | solution.py:180
  81.7 1.5 collective-permute-start.10
  83.1 10.5 %halves.3 = (f32[16,1,128,256]{3,2,1,0:T(8,128)}, bf16[8,1,128,256]{3,2,1,0:T(8,128)(2,1)S(1)}) custom-call(s32[6]{0:T(128)S(1)} %pad_add_fusion.1.info, s32[4,49]{1,0:T(4,128)S(1)} %pad_add_fusion.pairs, bf16[24,1,128,128]{3,2,1,0:T(8,128)(2,1)S(1)} %get-tuple-element.53.refs_0_, bf16[24,1,128,128]{3,2,1,0:T(8,128)(2,1)} %collective-permute-done.4.refs_1_, ...), custom_call_target="tpu_custom_call" | custom-call | flops 3221225472 | bytes 33554432 | tf_op jit(solution)/shard_map/halves/pallas_call | solution.py:180
  93.7 1.2 collective-permute-done.10
  94.8 4.9 %collective-permute-start.12 = (bf16[8,1,128,256]{3,2,1,0:T(8,128)(2,1)S(1)}, bf16[8,1,128,256]{3,2,1,0:T(8,128)(2,1)S(1)}, u32[]{:S(2)}, u32[]{:S(2)}) collective-permute-start(bf16[8,1,128,256]{3,2,1,0:T(8,128)(2,1)S(1)} %get-tuple-element.36), channel_id=1, source_target_pairs={{0,4},{1,5},{2,6},{3,7},{4,8},{5,9},{6,10},{7,11},{8,12},{9,13},{1... | collective-permute-start | bytes 1572872 | tf_op jit(solution)/shard_map/ppermute | solution.py:23
  99.8 0.1 add_convert_fusion.1
  99.9 1.3 collective-permute-start.11
  101.2 0.1 slice.76
  101.3 9.1 %collective-permute-done.12 = bf16[8,1,128,256]{3,2,1,0:T(8,128)(2,1)S(1)} collective-permute-done((bf16[8,1,128,256]{3,2,1,0:T(8,128)(2,1)S(1)}, bf16[8,1,128,256]{3,2,1,0:T(8,128)(2,1)S(1)}, u32[]{:S(2)}, u32[]{:S(2)}) %collective-permute-start.12) | collective-permute-done | bytes 524320 | tf_op jit(solution)/shard_map/ppermute | solution.py:23
  110.4 0.1 add_convert_fusion
  110.5 0.1 pad_maximum_fusion.2.refs_0_
  110.6 4.8 %collective-permute-done.11.refs_1_ = bf16[8,1,128,256]{3,2,1,0:T(8,128)(2,1)S(1)} collective-permute-done((bf16[8,1,128,256]{3,2,1,0:T(8,128)(2,1)S(1)}, bf16[8,1,128,256]{3,2,1,0:T(8,128)(2,1)S(1)}, u32[]{:S(2)}, u32[]{:S(2)}) %collective-permute-start.11) | collective-permute-done | bytes 524320 | tf_op jit(solution)/shard_map/ppermute | solution.py:23
  115.4 1.3 collective-permute-start.13
  116.7 0.1 slice.75
  116.7 0.1 pad_maximum_fusion.3.refs_0_
  116.8 7.5 %contract.3 = (f32[2,12,128,128]{3,2,1,0:T(8,128)S(1)}, f32[2,12,128,128]{3,2,1,0:T(8,128)S(1)}, f32[2,12,128,128]{3,2,1,0:T(8,128)}, f32[2,12,128,128]{3,2,1,0:T(8,128)}) custom-call(s32[6]{0:T(128)S(1)} %pad_add_fusion.1.info, s32[4,49]{1,0:T(4,128)S(1)} %pad_add_fusion.pairs, bf16[16,1,128,256]{3,2,1,0:T(8,128)(2,1)S(1)} %pad_maximum_fusion.3.refs_0_, ...), custom_call_target="tpu_custom_call" | custom-call | flops 1610612736 | bytes 16777216 | tf_op jit(solution)/shard_map/contract/pallas_call | solution.py:210
  124.4 1.2 copy-done.2
  125.5 4.0 %collective-permute-done.13.refs_1_ = bf16[8,1,128,256]{3,2,1,0:T(8,128)(2,1)S(1)} collective-permute-done((bf16[8,1,128,256]{3,2,1,0:T(8,128)(2,1)S(1)}, bf16[8,1,128,256]{3,2,1,0:T(8,128)(2,1)S(1)}, u32[]{:S(2)}, u32[]{:S(2)}) %collective-permute-start.13) | collective-permute-done | bytes 524320 | tf_op jit(solution)/shard_map/ppermute | solution.py:23
  129.5 4.6 %contract.4 = (f32[2,12,128,128]{3,2,1,0:T(8,128)S(1)}, bf16[2,12,128,128]{3,2,1,0:T(8,128)(2,1)S(1)}) custom-call(s32[6]{0:T(128)S(1)} %pad_add_fusion.1.info, s32[4,49]{1,0:T(4,128)S(1)} %pad_add_fusion.pairs, bf16[16,1,128,256]{3,2,1,0:T(8,128)(2,1)S(1)} %pad_maximum_fusion.2.refs_0_, bf16[8,1,128,256]{3,2,1,0:T(8,128)(2,1)S(1)} %collective-permute-done.13.refs_1_, ...), custom_call_target="tpu_custom_call" | custom-call | flops 1610612736 | bytes 16777216 | tf_op jit(solution)/shard_map/contract/pallas_call | solution.py:210
  134.1 0.1 collective-permute-start.14
  134.2 4.7 %contract.5 = (f32[2,12,128,128]{3,2,1,0:T(8,128)S(1)}, bf16[2,12,128,128]{3,2,1,0:T(8,128)(2,1)}) custom-call(s32[6]{0:T(128)S(1)} %pad_add_fusion.1.info, s32[4,49]{1,0:T(4,128)S(1)} %pad_add_fusion.pairs, bf16[16,1,128,256]{3,2,1,0:T(8,128)(2,1)S(1)} %pad_maximum_fusion.2.refs_0_, bf16[8,1,128,256]{3,2,1,0:T(8,128)(2,1)S(1)} %collective-permute-done.13.refs_1_, ...), custom_call_target="tpu_custom_call" | custom-call | flops 1610612736 | bytes 16777216 | tf_op jit(solution)/shard_map/contract/pallas_call | solution.py:210
  138.9 0.0 collective-permute-done.14
  138.9 0.9 copy-done.6
  139.8 0.5 collective-permute-start.17
  140.3 1.3 convert_add_fusion.1
  141.6 0.1 fusion.2
  141.7 1.4 collective-permute-start.15
  143.2 1.3 convert_add_fusion
  144.5 0.1 dynamic-slice_convert_fusion
  144.6 1.6 collective-permute-start.18
  146.2 6.8 %collective-permute-done.15 = bf16[12,128,128]{2,1,0:T(8,128)(2,1)} collective-permute-done((bf16[12,128,128]{2,1,0:T(8,128)(2,1)S(1)}, bf16[12,128,128]{2,1,0:T(8,128)(2,1)}, u32[]{:S(2)}, u32[]{:S(2)}) %collective-permute-start.15) | collective-permute-done | bytes 393248 | tf_op jit(solution)/shard_map/ppermute | solution.py:18
  152.9 1.3 fusion
  154.3 1.6 collective-permute-start.16
  155.9 0.0 collective-permute-done.18
  155.9 0.1 convert_add_fusion.2
  156.0 1.4 collective-permute-start.19
  157.4 2.9 %collective-permute-done.16 = bf16[12,64,128]{2,1,0:T(8,128)(2,1)S(1)} collective-permute-done((bf16[12,64,128]{2,1,0:T(8,128)(2,1)S(1)}, bf16[12,64,128]{2,1,0:T(8,128)(2,1)S(1)}, u32[]{:S(2)}, u32[]{:S(2)}) %collective-permute-start.16) | collective-permute-done | bytes 196640 | tf_op jit(solution)/shard_map/ppermute | solution.py:266
  160.4 1.4 collective-permute-done.19
  161.9 0.8 fusion.1
  (25 shorter events, 0.2 us)
Async XLA Ops:
  3.0 4.2 %copy-start = (bf16[512,512]{1,0:T(8,128)(2,1)S(1)}, bf16[512,512]{1,0:T(8,128)(2,1)}, u32[]{:S(2)}) copy-start(bf16[512,512]{1,0:T(8,128)(2,1)} %param.7) | copy-start | bytes 1572868
  3.0 4.3 %copy-start.7 = (s32[24,2]{0,1:T(2,128)S(1)}, s32[24,2]{0,1:T(2,128)}, u32[]{:S(2)}) copy-start(s32[24,2]{0,1:T(2,128)} %param.4) | copy-start | bytes 580
  4.3 51.3 %collective-permute-start.5 = (bf16[2,24,1,128,128]{4,3,1,2,0:T(8,128)(2,1)}, bf16[2,24,1,128,128]{4,3,1,2,0:T(8,128)(2,1)}, u32[]{:S(2)}, u32[]{:S(2)}) collective-permute-start(bf16[2,24,1,128,128]{4,3,1,2,0:T(8,128)(2,1)} %pad_maximum_fusion), channel_id=1, source_target_pairs={{0,2},{1,3},{2,0},{3,1},{4,6},{5,7},{6,4},{7,5},{8,10},{9,11},{10,... | collective-permute-start | bytes 4718600 | tf_op jit(solution)/shard_map/ppermute | solution.py:18
  7.2 45.9 %collective-permute-start = (bf16[4,128,512]{2,1,0:T(8,128)(2,1)S(1)}, bf16[4,128,512]{2,1,0:T(8,128)(2,1)S(1)}, u32[]{:S(2)}, u32[]{:S(2)}) collective-permute-start(bf16[4,128,512]{2,1,0:T(8,128)(2,1)S(1)} %bitcast.29), channel_id=1, source_target_pairs={{0,2},{1,3},{2,0},{3,1},{4,6},{5,7},{6,4},{7,5},{8,10},{9,11},{10,... | collective-permute-start | bytes 1572872 | tf_op jit(solution)/shard_map/ppermute | solution.py:18
  8.2 2.2 %collective-permute-start.1 = (s32[1,49]{1,0:T(1,128)S(1)}, s32[1,49]{1,0:T(1,128)S(1)}, u32[]{:S(2)}, u32[]{:S(2)}) collective-permute-start(s32[1,49]{1,0:T(1,128)S(1)} %add_bitcast_fusion), channel_id=1, source_target_pairs={{0,1},{1,0},{2,3},{3,2},{4,5},{5,4},{6,7},{7,6},{8,9},{9,8},{10,11... | collective-permute-start | bytes 596 | tf_op jit(solution)/shard_map/ppermute | solution.py:18
  8.2 44.9 %collective-permute-start.2 = (s32[1,49]{1,0:T(1,128)S(1)}, s32[1,49]{1,0:T(1,128)S(1)}, u32[]{:S(2)}, u32[]{:S(2)}) collective-permute-start(s32[1,49]{1,0:T(1,128)S(1)} %add_bitcast_fusion), channel_id=1, source_target_pairs={{0,2},{1,3},{2,0},{3,1},{4,6},{5,7},{6,4},{7,5},{8,10},{9,11},{10,... | collective-permute-start | bytes 596 | tf_op jit(solution)/shard_map/ppermute | solution.py:18
  10.3 42.9 %collective-permute-start.3 = (s32[1,49]{1,0:T(1,128)S(1)}, s32[1,49]{1,0:T(1,128)S(1)}, u32[]{:S(2)}, u32[]{:S(2)}) collective-permute-start(s32[1,49]{1,0:T(1,128)S(1)} %add_bitcast_fusion), channel_id=1, source_target_pairs={{0,3},{1,2},{2,1},{3,0},{4,7},{5,6},{6,5},{7,4},{8,11},{9,10},{10,... | collective-permute-start | bytes 596 | tf_op jit(solution)/shard_map/ppermute | solution.py:18
  10.3 59.0 %collective-permute-start.4 = (bf16[24,1,128,128]{3,2,1,0:T(8,128)(2,1)}, bf16[24,1,128,128]{3,2,1,0:T(8,128)(2,1)}, u32[]{:S(2)}, u32[]{:S(2)}) collective-permute-start(bf16[24,1,128,128]{3,2,1,0:T(8,128)(2,1)} %get-tuple-element.52), channel_id=1, source_target_pairs={{0,1},{1,0},{2,3},{3,2},{4,5},{5,4},{6,7},{7,6},{8,9},{9,8},{10,11... | collective-permute-start | bytes 2359304 | tf_op jit(solution)/shard_map/ppermute | solution.py:18
  53.2 15.8 %collective-permute-start.8 = (bf16[4,128,512]{2,1,0:T(8,128)(2,1)S(1)}, bf16[4,128,512]{2,1,0:T(8,128)(2,1)S(1)}, u32[]{:S(2)}, u32[]{:S(2)}) collective-permute-start(bf16[4,128,512]{2,1,0:T(8,128)(2,1)S(1)} %broadcast_select_fusion), channel_id=1, source_target_pairs={{4,0},{5,1},{6,2},{7,3},{8,4},{9,5},{10,6},{11,7},{12,8},{13,9},{1... | collective-permute-start | bytes 1572872 | tf_op jit(solution)/shard_map/ppermute | solution.py:23
  55.6 15.5 %collective-permute-start.7 = (bf16[2,4,128,512]{3,2,1,0:T(8,128)(2,1)}, bf16[2,4,128,512]{3,2,1,0:T(8,128)(2,1)}, u32[]{:S(2)}, u32[]{:S(2)}) collective-permute-start(bf16[2,4,128,512]{3,2,1,0:T(8,128)(2,1)} %pad_maximum_fusion.1), channel_id=1, source_target_pairs={{0,1},{1,0},{2,3},{3,2},{4,5},{5,4},{6,7},{7,6},{8,9},{9,8},{10,11... | collective-permute-start | bytes 3145736 | tf_op jit(solution)/shard_map/ppermute | solution.py:18
  58.1 13.1 %collective-permute-start.6 = (bf16[24,1,128,128]{3,2,1,0:T(8,128)(2,1)}, bf16[24,1,128,128]{3,2,1,0:T(8,128)(2,1)}, u32[]{:S(2)}, u32[]{:S(2)}) collective-permute-start(bf16[24,1,128,128]{3,2,1,0:T(8,128)(2,1)} %get-tuple-element.55), channel_id=1, source_target_pairs={{0,1},{1,0},{2,3},{3,2},{4,5},{5,4},{6,7},{7,6},{8,9},{9,8},{10,11... | collective-permute-start | bytes 2359304 | tf_op jit(solution)/shard_map/ppermute | solution.py:18
  69.1 2.0 %collective-permute-start.9 = (bf16[4,128,512]{2,1,0:T(8,128)(2,1)S(1)}, bf16[4,128,512]{2,1,0:T(8,128)(2,1)}, u32[]{:S(2)}, u32[]{:S(2)}) collective-permute-start(bf16[4,128,512]{2,1,0:T(8,128)(2,1)S(1)} %collective-permute-done.8.refs_7_), channel_id=1, source_target_pairs={{0,1},{1,0},{2,3},{3,2},{4,5},{5,4},{6,7},{7,6},{8,9},{9,8},{10,11... | collective-permute-start | bytes 1572872 | tf_op jit(solution)/shard_map/ppermute | solution.py:18
  81.6 18.1 %copy-start.4 = (f32[16,1,128,256]{3,2,1,0:T(8,128)S(1)}, f32[16,1,128,256]{3,2,1,0:T(8,128)}, u32[]{:S(2)}) copy-start(f32[16,1,128,256]{3,2,1,0:T(8,128)} %get-tuple-element.30) | copy-start | bytes 6291460
  81.7 13.2 %collective-permute-start.10 = (bf16[8,1,128,256]{3,2,1,0:T(8,128)(2,1)S(1)}, bf16[8,1,128,256]{3,2,1,0:T(8,128)(2,1)S(1)}, u32[]{:S(2)}, u32[]{:S(2)}) collective-permute-start(bf16[8,1,128,256]{3,2,1,0:T(8,128)(2,1)S(1)} %get-tuple-element.31), channel_id=1, source_target_pairs={{0,4},{1,5},{2,6},{3,7},{4,8},{5,9},{6,10},{7,11},{8,12},{9,13},{1... | collective-permute-start | bytes 1572872 | tf_op jit(solution)/shard_map/ppermute | solution.py:23
  93.7 7.6 %copy-start.5 = (f32[16,1,128,256]{3,2,1,0:T(8,128)S(1)}, f32[16,1,128,256]{3,2,1,0:T(8,128)}, u32[]{:S(2)}) copy-start(f32[16,1,128,256]{3,2,1,0:T(8,128)} %get-tuple-element.35) | copy-start | bytes 6291460
  94.8 15.5 %collective-permute-start.12 = (bf16[8,1,128,256]{3,2,1,0:T(8,128)(2,1)S(1)}, bf16[8,1,128,256]{3,2,1,0:T(8,128)(2,1)S(1)}, u32[]{:S(2)}, u32[]{:S(2)}) collective-permute-start(bf16[8,1,128,256]{3,2,1,0:T(8,128)(2,1)S(1)} %get-tuple-element.36), channel_id=1, source_target_pairs={{0,4},{1,5},{2,6},{3,7},{4,8},{5,9},{6,10},{7,11},{8,12},{9,13},{1... | collective-permute-start | bytes 1572872 | tf_op jit(solution)/shard_map/ppermute | solution.py:23
  99.9 15.5 %collective-permute-start.11 = (bf16[8,1,128,256]{3,2,1,0:T(8,128)(2,1)S(1)}, bf16[8,1,128,256]{3,2,1,0:T(8,128)(2,1)S(1)}, u32[]{:S(2)}, u32[]{:S(2)}) collective-permute-start(bf16[8,1,128,256]{3,2,1,0:T(8,128)(2,1)S(1)} %add_convert_fusion.1), channel_id=1, source_target_pairs={{4,0},{5,1},{6,2},{7,3},{8,4},{9,5},{10,6},{11,7},{12,8},{13,9},{1... | collective-permute-start | bytes 1572872 | tf_op jit(solution)/shard_map/ppermute | solution.py:23
  115.4 14.1 %collective-permute-start.13 = (bf16[8,1,128,256]{3,2,1,0:T(8,128)(2,1)S(1)}, bf16[8,1,128,256]{3,2,1,0:T(8,128)(2,1)S(1)}, u32[]{:S(2)}, u32[]{:S(2)}) collective-permute-start(bf16[8,1,128,256]{3,2,1,0:T(8,128)(2,1)S(1)} %add_convert_fusion), channel_id=1, source_target_pairs={{4,0},{5,1},{6,2},{7,3},{8,4},{9,5},{10,6},{11,7},{12,8},{13,9},{1... | collective-permute-start | bytes 1572872 | tf_op jit(solution)/shard_map/ppermute | solution.py:23
  124.3 1.2 copy-start.2
  129.5 4.7 %copy-start.1 = (f32[2,12,128,128]{3,2,1,0:T(8,128)S(1)}, f32[2,12,128,128]{3,2,1,0:T(8,128)}, u32[]{:S(2)}) copy-start(f32[2,12,128,128]{3,2,1,0:T(8,128)} %get-tuple-element.44.refs_2_) | copy-start | bytes 4718596
  134.1 4.8 %collective-permute-start.14 = (bf16[2,12,128,128]{3,2,1,0:T(8,128)(2,1)S(1)}, bf16[2,12,128,128]{3,2,1,0:T(8,128)(2,1)S(1)}, u32[]{:S(2)}, u32[]{:S(2)}) collective-permute-start(bf16[2,12,128,128]{3,2,1,0:T(8,128)(2,1)S(1)} %get-tuple-element.43), channel_id=1, source_target_pairs={{0,1},{1,0},{2,3},{3,2},{4,5},{5,4},{6,7},{7,6},{8,9},{9,8},{10,11... | collective-permute-start | bytes 2359304 | tf_op jit(solution)/shard_map/ppermute | solution.py:18
  138.9 0.9 copy-start.6
  139.8 3.3 %collective-permute-start.17 = (bf16[2,12,128,128]{3,2,1,0:T(8,128)(2,1)}, bf16[2,12,128,128]{3,2,1,0:T(8,128)(2,1)}, u32[]{:S(2)}, u32[]{:S(2)}) collective-permute-start(bf16[2,12,128,128]{3,2,1,0:T(8,128)(2,1)} %get-tuple-element.50), channel_id=1, source_target_pairs={{0,1},{1,0},{2,3},{3,2},{4,5},{5,4},{6,7},{7,6},{8,9},{9,8},{10,11... | collective-permute-start | bytes 2359304 | tf_op jit(solution)/shard_map/ppermute | solution.py:18
  141.6 2.9 %copy-start.3 = (f32[2,12,128,128]{3,2,1,0:T(8,128)}, f32[2,12,128,128]{3,2,1,0:T(8,128)S(1)}, u32[]{:S(2)}) copy-start(f32[2,12,128,128]{3,2,1,0:T(8,128)S(1)} %convert_add_fusion.1) | copy-start | bytes 4718596
  141.7 11.2 %collective-permute-start.15 = (bf16[12,128,128]{2,1,0:T(8,128)(2,1)S(1)}, bf16[12,128,128]{2,1,0:T(8,128)(2,1)}, u32[]{:S(2)}, u32[]{:S(2)}) collective-permute-start(bf16[12,128,128]{2,1,0:T(8,128)(2,1)S(1)} %fusion.2), channel_id=1, source_target_pairs={{0,2},{1,3},{2,0},{3,1},{4,6},{5,7},{6,4},{7,5},{8,10},{9,11},{10,... | collective-permute-start | bytes 1179656 | tf_op jit(solution)/shard_map/ppermute | solution.py:18
  144.6 11.3 %collective-permute-start.18 = (bf16[2,12,64,128]{3,2,1,0:T(8,128)(2,1)S(1)}, bf16[2,12,64,128]{3,2,1,0:T(8,128)(2,1)S(1)}, u32[]{:S(2)}, u32[]{:S(2)}) collective-permute-start(bf16[2,12,64,128]{3,2,1,0:T(8,128)(2,1)S(1)} %dynamic-slice_convert_fusion), channel_id=1, source_target_pairs={{0,16},{16,0},{1,17},{17,1},{2,18},{18,2},{3,19},{19,3},{4,20},{20... | collective-permute-start | bytes 1179656 | tf_op jit(solution)/shard_map/ppermute | solution.py:266
  154.3 6.1 %collective-permute-start.16 = (bf16[12,64,128]{2,1,0:T(8,128)(2,1)S(1)}, bf16[12,64,128]{2,1,0:T(8,128)(2,1)S(1)}, u32[]{:S(2)}, u32[]{:S(2)}) collective-permute-start(bf16[12,64,128]{2,1,0:T(8,128)(2,1)S(1)} %dynamic-slice_convert_fusion.1), channel_id=1, source_target_pairs={{0,16},{16,0},{1,17},{17,1},{2,18},{18,2},{3,19},{19,3},{4,20},{20... | collective-permute-start | bytes 589832 | tf_op jit(solution)/shard_map/ppermute | solution.py:266
  156.0 5.8 %collective-permute-start.19 = (bf16[12,64,128]{2,1,0:T(8,128)(2,1)S(1)}, bf16[12,64,128]{2,1,0:T(8,128)(2,1)S(1)}, u32[]{:S(2)}, u32[]{:S(2)}) collective-permute-start(bf16[12,64,128]{2,1,0:T(8,128)(2,1)S(1)} %fusion.4), channel_id=1, source_target_pairs={{0,2},{1,3},{2,0},{3,1},{4,6},{5,7},{6,4},{7,5},{8,10},{9,11},{10,... | collective-permute-start | bytes 589832 | tf_op jit(solution)/shard_map/ppermute | solution.py:18
